TPU v7x, 32 devices: a whole 2x2x4 slice. The times are simulated.
32 devices in a mesh: dp: 8 (over z, x), mp: 4 (over y, core).
Axes of the slice: x: 2, y: 2, z: 4, core: 2. Of those that a mesh axis runs over, the one named last changes fastest.
Arguments:
- tokens: bfloat16 [16, 664, 768], P('dp'), may hold values from -6 to 6
- cotangent: bfloat16 [16, 664, 768], P('dp'), may hold values from -6 to 6
- step_counts: int32 [16], P('dp'), may hold values from 1 to 2, as said below
- wrist_flags: int32 [16], P('dp'), may hold values 0 or 1
- inward_weight: float32 [3, 768, 768], P(None, 'dp', 'mp'), may hold values from -0.3125 to 0.3125
- outward_weight: float32 [768, 768], P('mp', 'dp'), may hold values from -0.875 to 0.875
- upward_weight: float32 [768, 3072], P('dp', 'mp')
- downward_weight: float32 [3072, 768], P('mp', 'dp'), may hold values from -0.109375 to 0.109375
- norm_table: float32 [4, 768], replicated
- momentum_inward: float32 [3, 768, 768], P(None, 'dp', 'mp'), may hold values from -0.00061035156 to 0.00061035156
- momentum_outward: float32 [768, 768], P('mp', 'dp'), may hold values from -0.00061035156 to 0.00061035156
- momentum_upward: float32 [768, 3072], P('dp', 'mp'), may hold values from -0.00061035156 to 0.00061035156
- momentum_downward: float32 [3072, 768], P('mp', 'dp'), may hold values from -0.00061035156 to 0.00061035156
- momentum_norms: float32 [4, 768], P(None, 'dp'), may hold values from -0.001953125 to 0.001953125
- variance_inward: float32 [3, 768, 768], P(None, 'dp', 'mp'), may hold values from 7.064254e-11 to 1.1302806e-09
- variance_outward: float32 [768, 768], P('mp', 'dp'), may hold values from 7.064254e-11 to 1.1302806e-09
- variance_upward: float32 [768, 3072], P('dp', 'mp'), may hold values from 7.064254e-11 to 1.1302806e-09
- variance_downward: float32 [3072, 768], P('mp', 'dp'), may hold values from 7.064254e-11 to 1.1302806e-09
- variance_norms: float32 [4, 768], P(None, 'dp'), may hold values from 6.3578287e-10 to 1.0172526e-08
Outputs:
- output: bfloat16 [16, 664, 768], P('dp')
- input_grad: float32 [16, 664, 768], P('dp')
- grad_norm: float32 [], replicated
- first_inward: float32 [3, 768, 768], P(None, 'dp', 'mp')
- second_inward: float32 [3, 768, 768], P(None, 'dp', 'mp')
- master_inward: float32 [3, 768, 768], P(None, 'dp', 'mp')
- first_outward: float32 [768, 768], P('mp', 'dp')
- second_outward: float32 [768, 768], P('mp', 'dp')
- master_outward: float32 [768, 768], P('mp', 'dp')
- first_upward: float32 [768, 3072], P('dp', 'mp')
- second_upward: float32 [768, 3072], P('dp', 'mp')
- master_upward: float32 [768, 3072], P('dp', 'mp')
- first_downward: float32 [3072, 768], P('mp', 'dp')
- second_downward: float32 [3072, 768], P('mp', 'dp')
- master_downward: float32 [3072, 768], P('mp', 'dp')
- first_norms: float32 [4, 768], P(None, 'dp')
- second_norms: float32 [4, 768], P(None, 'dp')
- master_norms: float32 [4, 768], P(None, 'dp')
Inputs may be any that keep to these rules, and one draw needn't show every extreme that they name: `step_counts`: some item has 2 timesteps and some item has 1.
All inputs are finite; a program needn't handle non-finite values. No bound on the sum of `wrist_flags` on one device may be relied on, other than what follows from the above.
Results may differ from a plain program's by a relative error of at most 0.012.
The roundings to bfloat16 on the way count: a program that leaves them out, or rounds other values in their place, can miss the bound.
Values may be sent and summed in bfloat16 or wider, within the bound.
A program may use at most 128 MiB of HBM per device.

v0:
```python
import jax
import jax.numpy as jnp
from jax import lax
from jax.sharding import PartitionSpec as P

HEAD_DIM = 64
TASK = 16
PRIMARY = 256
WRIST = 64
READOUT = 4
SLOTS = 664
MB = 2
STEP = 10


NORM_EPSILON = 1e-06
CLIP_NORM = 1.0
BETA_ONE = 0.9
BETA_TWO = 0.999
ADAM_EPSILON = 1e-08
WEIGHT_DECAY = 0.1
NEGATIVE = -1e30
RATE_INWARD = 0.05
RATE_OUTWARD = 0.15
RATE_UPWARD = 0.04
RATE_DOWNWARD = 0.02
RATE_NORMS = 0.5


def slot_mask(live_steps, has_wrist):
    position = jnp.arange(SLOTS, dtype=jnp.int32)
    relative = position - TASK
    period = PRIMARY + WRIST + READOUT
    is_task = relative < 0
    forward_pos = jnp.maximum(relative, 0)
    stepno = forward_pos // period
    offset = forward_pos % period
    not_task = jnp.logical_not(is_task)
    is_read = jnp.logical_and(not_task, offset >= PRIMARY + WRIST)
    is_obs = jnp.logical_and(not_task, jnp.logical_not(is_read))
    is_wrist = jnp.logical_and(is_obs, offset >= PRIMARY)
    present = jnp.logical_or(
        is_task,
        jnp.logical_and(
            stepno < live_steps, jnp.logical_or(jnp.logical_not(is_wrist), has_wrist == 1)
        ),
    )
    see_obs = is_obs[None, :] & not_task[:, None] & (stepno[None, :] <= stepno[:, None])
    see_read = is_read[None, :] & is_read[:, None] & (stepno[None, :] == stepno[:, None])
    return present[None, :] & (is_task[None, :] | see_obs | see_read)


def layer_stats(values):
    centre = values - jnp.mean(values, axis=-1, keepdims=True)
    inverse = lax.rsqrt(jnp.mean(centre * centre, axis=-1, keepdims=True) + NORM_EPSILON)
    return (centre * inverse, inverse)


def layer_back(grad_result, normal, inverse, gain_row):
    scaled = grad_result * gain_row
    return inverse * (
        scaled
        - jnp.mean(scaled, axis=-1, keepdims=True)
        - normal * jnp.mean(scaled * normal, axis=-1, keepdims=True)
    )


def gelu_tanh(values):
    return (
        0.5
        * values
        * (1.0 + jnp.tanh(0.7978845608028654 * (values + 0.044715 * values * values * values)))
    )


def attention_scores(queries, key_heads, allowed, score_scale):
    dotted = (
        jnp.einsum("nqhd,nkhd->nhqk", queries, key_heads, preferred_element_type=jnp.float32)
        * score_scale
    )
    return jnp.where(allowed, dotted, NEGATIVE)


def adam_update(master, momentum, variance, gradient, clip_scale, step_rate, decay_rate):
    clipped = gradient * clip_scale
    moment_one = BETA_ONE * momentum + (1.0 - BETA_ONE) * clipped
    moment_two = BETA_TWO * variance + (1.0 - BETA_TWO) * clipped * clipped
    first_hat = moment_one / (1.0 - BETA_ONE**STEP)
    second_hat = moment_two / (1.0 - BETA_TWO**STEP)
    updated = master - step_rate * (
        first_hat / (jnp.sqrt(second_hat) + ADAM_EPSILON) + decay_rate * master
    )
    return (moment_one, moment_two, updated)


def body(
    tokens,
    cotangent,
    step_counts,
    wrist_flags,
    inward_weight,
    outward_weight,
    upward_weight,
    downward_weight,
    norm_table,
    momentum_inward,
    momentum_outward,
    momentum_upward,
    momentum_downward,
    momentum_norms,
    variance_inward,
    variance_outward,
    variance_upward,
    variance_downward,
    variance_norms,
):
    full_inward, full_outward, full_upward, full_downward = (
        lax.all_gather(inward_weight.astype(jnp.bfloat16), "dp", axis=1, tiled=True),
        lax.all_gather(outward_weight.astype(jnp.bfloat16), "dp", axis=1, tiled=True),
        lax.all_gather(upward_weight.astype(jnp.bfloat16), "dp", axis=0, tiled=True),
        lax.all_gather(downward_weight.astype(jnp.bfloat16), "dp", axis=1, tiled=True),
    )
    model_width = norm_table.shape[1]
    local_heads = full_inward.shape[2] // HEAD_DIM
    score_scale = HEAD_DIM ** (-0.5)
    per_batch = tokens.shape[0] // MB
    row_count = per_batch * SLOTS
    share_rows = row_count // lax.axis_size("mp")
    share_start = lax.axis_index("mp") * share_rows
    results = []
    input_grads = []
    local_sums = None
    for batch_index in range(MB):
        start_item = batch_index * per_batch
        block_tokens = (
            tokens[start_item : start_item + per_batch]
            .astype(jnp.float32)
            .reshape(row_count, model_width)
        )
        block_back = (
            cotangent[start_item : start_item + per_batch]
            .astype(jnp.float32)
            .reshape(row_count, model_width)
        )
        allowed = jax.vmap(slot_mask)(
            step_counts[start_item : start_item + per_batch],
            wrist_flags[start_item : start_item + per_batch],
        )[:, None]
        normal_one, inverse_one = layer_stats(block_tokens)
        normed_one = (normal_one * norm_table[0] + norm_table[1]).astype(jnp.bfloat16)
        projected = jnp.einsum(
            "rd,cdm->crm", normed_one, full_inward, preferred_element_type=jnp.float32
        ).astype(jnp.bfloat16)
        triple = projected.reshape(3, per_batch, SLOTS, local_heads, HEAD_DIM)
        queries = triple[0]
        key_heads = triple[1]
        value_heads = triple[2]
        scores = attention_scores(queries, key_heads, allowed, score_scale)
        highest = jnp.max(scores, axis=-1, keepdims=True)
        log_total = highest + jnp.log(jnp.sum(jnp.exp(scores - highest), axis=-1, keepdims=True))
        attention_low = jnp.exp(scores - log_total).astype(jnp.bfloat16)
        context = (
            jnp.einsum(
                "nhqk,nkhd->nqhd", attention_low, value_heads, preferred_element_type=jnp.float32
            )
            .astype(jnp.bfloat16)
            .reshape(row_count, -1)
        )
        attn_terms = jnp.dot(context, full_outward, preferred_element_type=jnp.float32)
        tokens_share = lax.dynamic_slice_in_dim(block_tokens, share_start, share_rows, 0)
        back_share = lax.dynamic_slice_in_dim(block_back, share_start, share_rows, 0)
        middle_share = tokens_share + lax.psum_scatter(
            attn_terms, "mp", scatter_dimension=0, tiled=True
        )
        normal_two, inverse_two = layer_stats(middle_share)
        normed_share = (normal_two * norm_table[2] + norm_table[3]).astype(jnp.bfloat16)
        normed_two = lax.all_gather(normed_share, "mp", axis=0, tiled=True)
        upper_pre = jnp.dot(normed_two, full_upward, preferred_element_type=jnp.float32)
        hidden = gelu_tanh(upper_pre).astype(jnp.bfloat16)
        lowered_share = lax.psum_scatter(
            jnp.dot(hidden, full_downward, preferred_element_type=jnp.float32).astype(jnp.bfloat16),
            "mp",
            scatter_dimension=0,
            tiled=True,
        ).astype(jnp.float32)
        output_share = (middle_share + lowered_share).astype(jnp.bfloat16)
        back_rows = block_back.astype(jnp.bfloat16)
        grad_down = jnp.einsum("rf,rd->fd", hidden, back_rows, preferred_element_type=jnp.float32)
        grad_hidden = jnp.einsum(
            "rd,fd->rf", back_rows, full_downward, preferred_element_type=jnp.float32
        )
        upper_pull = jax.vjp(gelu_tanh, upper_pre)[1]
        grad_upper = upper_pull(grad_hidden)[0].astype(jnp.bfloat16)
        grad_up = jnp.einsum(
            "rd,rf->df", normed_two, grad_upper, preferred_element_type=jnp.float32
        )
        normed_terms = jnp.einsum(
            "rf,df->rd", grad_upper, full_upward, preferred_element_type=jnp.float32
        )
        grad_normed_two = lax.psum_scatter(normed_terms, "mp", scatter_dimension=0, tiled=True)
        gain_two = jnp.sum(grad_normed_two * normal_two, axis=0)
        shift_two = jnp.sum(grad_normed_two, axis=0)
        grad_middle_share = back_share + layer_back(
            grad_normed_two, normal_two, inverse_two, norm_table[2]
        )
        middle_low, output_rows = (
            lax.all_gather(grad_middle_share.astype(jnp.bfloat16), "mp", axis=0, tiled=True),
            lax.all_gather(output_share, "mp", axis=0, tiled=True),
        )
        results.append(output_rows.reshape(per_batch, SLOTS, model_width))
        grad_out = jnp.einsum("rm,rd->md", context, middle_low, preferred_element_type=jnp.float32)
        grad_context = (
            jnp.einsum("rd,md->rm", middle_low, full_outward, preferred_element_type=jnp.float32)
            .astype(jnp.bfloat16)
            .reshape(per_batch, SLOTS, local_heads, HEAD_DIM)
        )
        scores_again = attention_scores(queries, key_heads, allowed, score_scale)
        attention_full = jnp.exp(scores_again - log_total)
        attention_again = attention_full.astype(jnp.bfloat16)
        grad_values = jnp.einsum(
            "nhqk,nqhd->nkhd", attention_again, grad_context, preferred_element_type=jnp.float32
        ).astype(jnp.bfloat16)
        grad_weights = jnp.einsum(
            "nqhd,nkhd->nhqk", grad_context, value_heads, preferred_element_type=jnp.float32
        )
        grad_scores = (
            attention_full
            * (grad_weights - jnp.sum(grad_weights * attention_full, axis=-1, keepdims=True))
        ).astype(jnp.bfloat16)
        grad_queries = (
            jnp.einsum(
                "nhqk,nkhd->nqhd", grad_scores, key_heads, preferred_element_type=jnp.float32
            )
            * score_scale
        ).astype(jnp.bfloat16)
        grad_keys = (
            jnp.einsum("nhqk,nqhd->nkhd", grad_scores, queries, preferred_element_type=jnp.float32)
            * score_scale
        ).astype(jnp.bfloat16)
        grad_triple = jnp.stack([grad_queries, grad_keys, grad_values]).reshape(3, row_count, -1)
        grad_in = jnp.einsum(
            "rd,crm->cdm", normed_one, grad_triple, preferred_element_type=jnp.float32
        )
        first_terms = jnp.einsum(
            "crm,cdm->rd", grad_triple, full_inward, preferred_element_type=jnp.float32
        )
        grad_normed_one = lax.psum_scatter(first_terms, "mp", scatter_dimension=0, tiled=True)
        normal_share = lax.dynamic_slice_in_dim(normal_one, share_start, share_rows, 0)
        inverse_share = lax.dynamic_slice_in_dim(inverse_one, share_start, share_rows, 0)
        gain_one = jnp.sum(grad_normed_one * normal_share, axis=0)
        shift_one = jnp.sum(grad_normed_one, axis=0)
        tokens_grad_share = grad_middle_share + layer_back(
            grad_normed_one, normal_share, inverse_share, norm_table[0]
        )
        table_terms = jnp.stack([gain_one, shift_one, gain_two, shift_two])[None]
        grad_tokens, gathered_tables = (
            lax.all_gather(tokens_grad_share, "mp", axis=0, tiled=True),
            lax.all_gather(table_terms, "mp", axis=0, tiled=True),
        )
        grad_table = jnp.sum(gathered_tables, axis=0)
        input_grads.append(grad_tokens.reshape(per_batch, SLOTS, model_width))
        batch_grads = (grad_in, grad_out, grad_up, grad_down, grad_table)
        if local_sums is None:
            local_sums = batch_grads
        else:
            local_sums = tuple((former + latter for former, latter in zip(local_sums, batch_grads)))
    shards = (
        lax.psum_scatter(local_sums[0], "dp", scatter_dimension=1, tiled=True),
        lax.psum_scatter(local_sums[1], "dp", scatter_dimension=1, tiled=True),
        lax.psum_scatter(local_sums[2], "dp", scatter_dimension=0, tiled=True),
        lax.psum_scatter(local_sums[3], "dp", scatter_dimension=1, tiled=True),
        lax.psum_scatter(local_sums[4], "dp", scatter_dimension=1, tiled=True),
    )
    mp_count = lax.axis_size("mp")
    squares = (
        sum((jnp.sum(piece * piece) for piece in shards[:4]))
        + jnp.sum(shards[4] * shards[4]) / mp_count
    )
    grad_norm = jnp.sqrt(lax.psum(squares, ("dp", "mp")))
    clip_scale = jnp.minimum(1.0, CLIP_NORM / (grad_norm + 1e-06))
    shard_width = shards[4].shape[1]
    own_table = lax.dynamic_slice_in_dim(
        norm_table, lax.axis_index("dp") * shard_width, shard_width, 1
    )
    inward_new = adam_update(
        inward_weight,
        momentum_inward,
        variance_inward,
        shards[0],
        clip_scale,
        RATE_INWARD,
        WEIGHT_DECAY,
    )
    outward_new = adam_update(
        outward_weight,
        momentum_outward,
        variance_outward,
        shards[1],
        clip_scale,
        RATE_OUTWARD,
        WEIGHT_DECAY,
    )
    upward_new = adam_update(
        upward_weight,
        momentum_upward,
        variance_upward,
        shards[2],
        clip_scale,
        RATE_UPWARD,
        WEIGHT_DECAY,
    )
    downward_new = adam_update(
        downward_weight,
        momentum_downward,
        variance_downward,
        shards[3],
        clip_scale,
        RATE_DOWNWARD,
        WEIGHT_DECAY,
    )
    norms_new = adam_update(
        own_table, momentum_norms, variance_norms, shards[4], clip_scale, RATE_NORMS, 0.0
    )
    output = jnp.concatenate(results, axis=0)
    input_grad = jnp.concatenate(input_grads, axis=0)
    return (
        output,
        input_grad,
        grad_norm,
        inward_new[0],
        inward_new[1],
        inward_new[2],
        outward_new[0],
        outward_new[1],
        outward_new[2],
        upward_new[0],
        upward_new[1],
        upward_new[2],
        downward_new[0],
        downward_new[1],
        downward_new[2],
        norms_new[0],
        norms_new[1],
        norms_new[2],
    )


def solution(mesh):
    placed = (
        P("dp", None, None),
        P("dp", None, None),
        P("dp"),
        P("dp"),
        P(None, "dp", "mp"),
        P("mp", "dp"),
        P("dp", "mp"),
        P("mp", "dp"),
        P(),
        P(None, "dp", "mp"),
        P("mp", "dp"),
        P("dp", "mp"),
        P("mp", "dp"),
        P(None, "dp"),
        P(None, "dp", "mp"),
        P("mp", "dp"),
        P("dp", "mp"),
        P("mp", "dp"),
        P(None, "dp"),
    )
    return jax.shard_map(
        body,
        mesh=mesh,
        in_specs=placed,
        out_specs=(
            P("dp", None, None),
            P("dp", None, None),
            P(),
            P(None, "dp", "mp"),
            P(None, "dp", "mp"),
            P(None, "dp", "mp"),
            P("mp", "dp"),
            P("mp", "dp"),
            P("mp", "dp"),
            P("dp", "mp"),
            P("dp", "mp"),
            P("dp", "mp"),
            P("mp", "dp"),
            P("mp", "dp"),
            P("mp", "dp"),
            P(None, "dp"),
            P(None, "dp"),
            P(None, "dp"),
        ),
        check_vma=False,
    )
```

profile of v0, /device:TPU:0, one launch (start us, length us, event | category | flops | bytes accessed | tf_op | source)
XLA Modules:
  0.0 873.5 jit_solution(11266263418255840006)
XLA Ops:
  16.2 33.8 %all_gather.43 = bf16[192,768]{0,1:T(8,128)(2,1)S(1)} all-gather(bf16[192,96]{0,1:T(8,128)(2,1)S(1)} %copy.97), channel_id=1, replica_groups=mesh['dp'=8,'mp'=4] {'dp'}, dimensions={1}, use_global_device_ids=true | all-gather | bytes 331776 | tf_op jit(solution)/shard_map/all_gather | solution.py:119
  50.0 38.9 %all_gather.42 = bf16[3,768,192]{2,0,1:T(4,128)(2,1)} all-gather(bf16[3,96,192]{2,0,1:T(4,128)(2,1)S(1)} %copy.94), channel_id=1, replica_groups=mesh['dp'=8,'mp'=4] {'dp'}, dimensions={1}, use_global_device_ids=true | all-gather | bytes 995328 | tf_op jit(solution)/shard_map/all_gather | solution.py:118
  110.7 40.1 %fusion.86 = (f32[168,768]{1,0:T(8,128)}, f32[168,768]{1,0:T(8,128)}) fusion(f32[664,768]{1,0:T(8,128)} %fusion.102, f32[664,768]{1,0:T(8,128)} %fusion.100), kind=kCustom, calls=%all-reduce-scatter.10 | all-reduce-scatter fusion | flops 1032193 | bytes 5112320
  153.7 3.2 collective-permute-start.2
  169.7 9.7 %all-gather.2 = bf16[4,166,768]{2,1,0:T(8,128)(2,1)S(1)} all-gather(bf16[1,166,768]{2,1,0:T(8,128)(2,1)S(1)} %get-tuple-element.167), channel_id=1, replica_groups=mesh['dp'=8,'mp'=4] {'mp'}, dimensions={0}, use_global_device_ids=true | all-gather | bytes 1274880 | tf_op jit(solution)/shard_map/all_gather | solution.py:177
  180.7 10.0 %all-gather.4 = bf16[4,166,768]{2,1,0:T(8,128)(2,1)S(1)} all-gather(bf16[1,166,768]{2,1,0:T(8,128)(2,1)S(1)} %get-tuple-element.168), channel_id=1, replica_groups=mesh['dp'=8,'mp'=4] {'mp'}, dimensions={0}, use_global_device_ids=true | all-gather | bytes 1274880 | tf_op jit(solution)/shard_map/all_gather | solution.py:177
  192.0 4.0 fusion.103
  198.3 4.3 convolution_convert_fusion
  205.0 22.4 %fusion.87 = (bf16[168,768]{1,0:T(8,128)(2,1)S(1)}, bf16[168,768]{1,0:T(8,128)(2,1)S(1)}) fusion(bf16[664,768]{1,0:T(8,128)(2,1)} %convolution_convert_fusion, bf16[664,768]{1,0:T(8,128)(2,1)} %convolution_convert_fusion.1), kind=kCustom, calls=%all-reduce-scatter.11 | all-reduce-scatter fusion | flops 1032193 | bytes 2556416
  232.4 4.4 fusion.19
  244.0 39.4 %fusion.85 = (f32[168,768]{1,0:T(8,128)S(1)}, f32[168,768]{1,0:T(8,128)S(1)}) fusion(f32[664,768]{1,0:T(8,128)} %fusion.105, f32[664,768]{1,0:T(8,128)} %fusion.104), kind=kCustom, calls=%all-reduce-scatter.9 | all-reduce-scatter fusion | flops 1032193 | bytes 5112320
  290.9 3.9 concatenate.11
  301.1 3.3 convert_bitcast_fusion.3
  304.4 10.2 %all-gather.6 = bf16[4,166,768]{2,1,0:T(8,128)(2,1)} all-gather(bf16[1,166,768]{2,1,0:T(8,128)(2,1)S(1)} %get-tuple-element.145), channel_id=1, replica_groups=mesh['dp'=8,'mp'=4] {'mp'}, dimensions={0}, use_global_device_ids=true | all-gather | bytes 1274880 | tf_op jit(solution)/shard_map/all_gather | solution.py:207
  319.0 5.3 convolution_convert_fusion.4
  333.1 10.8 %all-gather.8 = bf16[4,166,768]{2,1,0:T(8,128)(2,1)} all-gather(bf16[1,166,768]{2,1,0:T(8,128)(2,1)S(1)} %get-tuple-element.147), channel_id=1, replica_groups=mesh['dp'=8,'mp'=4] {'mp'}, dimensions={0}, use_global_device_ids=true | all-gather | bytes 1274880 | tf_op jit(solution)/shard_map/all_gather | solution.py:207
  348.5 4.6 convolution_convert_fusion.2
  364.4 39.4 %fusion.84 = (f32[168,768]{1,0:T(8,128)S(1)}, f32[168,768]{1,0:T(8,128)S(1)}) fusion(f32[664,768]{1,0:T(8,128)} %convolution_bitcast_fusion, f32[664,768]{1,0:T(8,128)} %convolution_bitcast_fusion.1), kind=kCustom, calls=%all-reduce-scatter.8 | all-reduce-scatter fusion | flops 1032193 | bytes 5112320
  405.1 3.4 collective-permute-start.7
  413.4 5.3 all-gather.11
  418.8 5.5 all-gather.10
  459.6 10.2 %all-gather.5 = bf16[4,166,768]{2,1,0:T(8,128)(2,1)S(1)} all-gather(bf16[1,166,768]{2,1,0:T(8,128)(2,1)S(1)} %copy-done.44), channel_id=1, replica_groups=mesh['dp'=8,'mp'=4] {'mp'}, dimensions={0}, use_global_device_ids=true | all-gather | bytes 1274880 | tf_op jit(solution)/shard_map/all_gather | solution.py:208
  470.0 10.4 %all-gather.3 = bf16[4,166,768]{2,1,0:T(8,128)(2,1)S(1)} all-gather(bf16[1,166,768]{2,1,0:T(8,128)(2,1)S(1)} %copy-done.43), channel_id=1, replica_groups=mesh['dp'=8,'mp'=4] {'mp'}, dimensions={0}, use_global_device_ids=true | all-gather | bytes 1274880 | tf_op jit(solution)/shard_map/all_gather | solution.py:208
  482.1 3.9 reduce-scatter.36.cloned.1.call-done
  488.1 62.5 %reduce-scatter.34.cloned.1.call-done = f32[96,192]{1,0:T(8,128)} async-done(((f32[768,192]{1,0:T(8,128)}), f32[96,192]{1,0:T(8,128)}) %reduce-scatter.34.cloned.1.call-update) | async-done | bytes 73744
  552.2 21.3 %all-gather.21.cloned.1.call-done = f32[4,166,768]{2,1,0:T(8,128)} async-done(((f32[1,166,768]{2,1,0:T(8,128)}), f32[4,166,768]{2,1,0:T(8,128)}) %all-gather.21.cloned.1.call-update) | async-done | bytes 2039824 | tf_op jit(solution)/shard_map/all_gather | solution.py:257
  575.3 22.1 %all-gather.23.cloned.1.call-done = f32[4,166,768]{2,1,0:T(8,128)} async-done(((f32[1,166,768]{2,1,0:T(8,128)}), f32[4,166,768]{2,1,0:T(8,128)}) %all-gather.23.cloned.1.call-update) | async-done | bytes 2039824 | tf_op jit(solution)/shard_map/all_gather | solution.py:257
  600.5 67.6 %reduce-scatter.32.cloned.1.call-done = f32[96,576]{1,0:T(8,128)} async-done(((f32[768,576]{1,0:T(8,128)}), f32[96,576]{1,0:T(8,128)}) %reduce-scatter.32.cloned.1.call-update) | async-done | bytes 221200
  671.4 68.6 %reduce-scatter.28.cloned.1.call-done = f32[96,768]{1,0:T(8,128)} async-done(((f32[768,768]{1,0:T(8,128)}), f32[96,768]{1,0:T(8,128)}) %reduce-scatter.28.cloned.1.call-update) | async-done | bytes 294928 | tf_op jit(solution)/shard_map/reduce_scatter | solution.py:270
  742.3 69.2 %reduce-scatter.30.cloned.1.call-done = f32[768,96]{0,1:T(8,128)} async-done(((f32[768,768]{0,1:T(8,128)}), f32[768,96]{0,1:T(8,128)}) %reduce-scatter.30.cloned.1.call-update) | async-done | bytes 294928 | tf_op jit(solution)/shard_map/reduce_scatter | solution.py:271
  813.9 3.9 pad_maximum_fusion
  817.7 39.4 %psum.7 = f32[]{:T(128)} all-reduce(f32[]{:T(128)S(6)} %add.403), channel_id=1, replica_groups=mesh['dp'=8,'mp'=4] {'dp','mp'}, use_global_device_ids=true, to_apply=%region_50.51 | all-reduce | flops 1 | bytes 8 | tf_op jit(solution)/shard_map/psum | solution.py:279
  (366 shorter events, 169.5 us)
Async XLA Ops:
  7.2 184.8 %all-gather.17.cloned.1.call-start = ((), (), s32[]{:S(2)}) async-start(), calls=%async_computation.5 | async-start | bytes 1327104 | tf_op jit(solution)/shard_map/all_gather | solution.py:120
  9.0 189.2 %all-gather.19.cloned.1.call-start = ((), (), s32[]{:S(2)}) async-start(), calls=%async_computation.6 | async-start | bytes 1327104 | tf_op jit(solution)/shard_map/all_gather | solution.py:121
  15.9 76.8 %copy-start.67 = (f32[768]{0:T(1024)}, f32[768]{0:T(1024)S(1)}, u32[]{:S(2)}) copy-start(f32[768]{0:T(1024)S(1)} %get-tuple-element.111) | copy-start | bytes 9220
  50.0 58.3 %copy-start.4 = (bf16[192,768]{0,1:T(8,128)(2,1)}, bf16[192,768]{0,1:T(8,128)(2,1)S(1)}, u32[]{:S(2)}) copy-start(bf16[192,768]{0,1:T(8,128)(2,1)S(1)} %all_gather.43) | copy-start | bytes 884740
  92.8 13.7 %copy-start.23 = (bf16[1,664,192]{1,2,0:T(8,128)(2,1)}, bf16[1,664,192]{1,2,0:T(8,128)(2,1)S(1)}, u32[]{:S(2)}) copy-start(bf16[1,664,192]{1,2,0:T(8,128)(2,1)S(1)} %get-tuple-element.164) | copy-start | bytes 764932
  110.7 46.1 %copy-start.28 = (f32[768,96]{0,1:T(8,128)S(1)}, f32[768,96]{0,1:T(8,128)}, u32[]{:S(2)}) copy-start(f32[768,96]{0,1:T(8,128)} %param.26) | copy-start | bytes 884740
  151.6 12.0 %collective-permute-start = (f32[6,768]{1,0:T(8,128)S(1)}, f32[6,768]{1,0:T(8,128)S(1)}, u32[]{:S(2)}, u32[]{:S(2)}) collective-permute-start(f32[6,768]{1,0:T(8,128)S(1)} %slice.92), channel_id=1, source_target_pairs={{0,1},{1,2},{2,3},{4,5},{5,6},{6,7},{8,9},{9,10},{10,11},{12,13},{... | collective-permute-start | bytes 55304
  153.7 13.9 %collective-permute-start.2 = (f32[6,768]{1,0:T(8,128)S(1)}, f32[6,768]{1,0:T(8,128)S(1)}, u32[]{:S(2)}, u32[]{:S(2)}) collective-permute-start(f32[6,768]{1,0:T(8,128)S(1)} %slice.94), channel_id=1, source_target_pairs={{0,1},{1,2},{2,3},{4,5},{5,6},{6,7},{8,9},{9,10},{10,11},{12,13},{... | collective-permute-start | bytes 55304
  157.6 328.4 %reduce-scatter.36.cloned.1.call-start = ((), (), s32[]{:S(2)}) async-start(), calls=%async_computation.13 | async-start | bytes 442368
  169.4 131.7 %copy-start.64 = (f32[166]{0:T(256)}, f32[166]{0:T(256)S(1)}, u32[]{:S(2)}) copy-start(f32[166]{0:T(256)S(1)} %add_rsqrt_fusion.2) | copy-start | bytes 1996
  227.5 63.4 %collective-permute-start.1 = (bf16[6,768]{1,0:T(8,128)(2,1)S(1)}, bf16[6,768]{1,0:T(8,128)(2,1)}, u32[]{:S(2)}, u32[]{:S(2)}) collective-permute-start(bf16[6,768]{1,0:T(8,128)(2,1)S(1)} %slice.93), channel_id=1, source_target_pairs={{0,1},{1,2},{2,3},{4,5},{5,6},{6,7},{8,9},{9,10},{10,11},{12,13},{... | collective-permute-start | bytes 27656
  229.6 65.2 %collective-permute-start.3 = (bf16[6,768]{1,0:T(8,128)(2,1)S(1)}, bf16[6,768]{1,0:T(8,128)(2,1)S(1)}, u32[]{:S(2)}, u32[]{:S(2)}) collective-permute-start(bf16[6,768]{1,0:T(8,128)(2,1)S(1)} %slice.95), channel_id=1, source_target_pairs={{0,1},{1,2},{2,3},{4,5},{5,6},{6,7},{8,9},{9,10},{10,11},{12,13},{... | collective-permute-start | bytes 27656
  283.4 14.1 %collective-permute-start.4 = (f32[6,768]{1,0:T(8,128)S(1)}, f32[6,768]{1,0:T(8,128)S(1)}, u32[]{:S(2)}, u32[]{:S(2)}) collective-permute-start(f32[6,768]{1,0:T(8,128)S(1)} %slice.96), channel_id=1, source_target_pairs={{0,1},{1,2},{2,3},{4,5},{5,6},{6,7},{8,9},{9,10},{10,11},{12,13},{... | collective-permute-start | bytes 55304
  287.8 11.2 %collective-permute-start.6 = (f32[6,768]{1,0:T(8,128)S(1)}, f32[6,768]{1,0:T(8,128)S(1)}, u32[]{:S(2)}, u32[]{:S(2)}) collective-permute-start(f32[6,768]{1,0:T(8,128)S(1)} %slice.98), channel_id=1, source_target_pairs={{0,1},{1,2},{2,3},{4,5},{5,6},{6,7},{8,9},{9,10},{10,11},{12,13},{... | collective-permute-start | bytes 55304
  333.1 13.6 %copy-start.5 = (bf16[192,768]{0,1:T(8,128)(2,1)S(1)}, bf16[192,768]{0,1:T(8,128)(2,1)}, u32[]{:S(2)}) copy-start(bf16[192,768]{0,1:T(8,128)(2,1)} %copy-done.4) | copy-start | bytes 884740
  364.4 44.1 %copy-start.7 = (bf16[664,768]{1,0:T(8,128)(2,1)S(1)}, bf16[664,768]{1,0:T(8,128)(2,1)}, u32[]{:S(2)}) copy-start(bf16[664,768]{1,0:T(8,128)(2,1)} %reshape.865) | copy-start | bytes 3059716
  364.4 44.1 %copy-start.39 = (bf16[3,64,664]{2,1,0:T(8,128)(2,1)S(1)}, bf16[3,64,664]{2,1,0:T(8,128)(2,1)}, u32[]{:S(2)}) copy-start(bf16[3,64,664]{2,1,0:T(8,128)(2,1)} %copy-done.38) | copy-start | bytes 764932
  403.8 5.2 collective-permute-start.5
  405.1 4.3 collective-permute-start.7
  409.4 15.9 %copy-start.6 = (bf16[664,768]{1,0:T(8,128)(2,1)S(1)}, bf16[664,768]{1,0:T(8,128)(2,1)}, u32[]{:S(2)}) copy-start(bf16[664,768]{1,0:T(8,128)(2,1)} %reshape.869) | copy-start | bytes 3059716
  409.4 15.9 %copy-start.35 = (bf16[3,64,664]{2,1,0:T(8,128)(2,1)S(1)}, bf16[3,64,664]{2,1,0:T(8,128)(2,1)}, u32[]{:S(2)}) copy-start(bf16[3,64,664]{2,1,0:T(8,128)(2,1)} %copy-done.34) | copy-start | bytes 764932
  425.3 125.3 %reduce-scatter.34.cloned.1.call-start = ((), (), s32[]{:S(2)}) async-start(), calls=%async_computation.12 | async-start | bytes 884736
  428.8 144.7 %all-gather.21.cloned.1.call-start = ((), (), s32[]{:S(2)}) async-start(), calls=%async_computation.9 | async-start | bytes 2580480 | tf_op jit(solution)/shard_map/all_gather | solution.py:257
  432.4 165.0 %all-gather.23.cloned.1.call-start = ((), (), s32[]{:S(2)}) async-start(), calls=%async_computation.10 | async-start | bytes 2580480 | tf_op jit(solution)/shard_map/all_gather | solution.py:257
  433.0 235.1 %reduce-scatter.32.cloned.1.call-start = ((), (), s32[]{:S(2)}) async-start(), calls=%async_computation.11 | async-start | bytes 2211840
  443.7 296.3 %reduce-scatter.28.cloned.1.call-start = ((), (), s32[]{:S(2)}) async-start(), calls=%async_computation.7 | async-start | bytes 2654208 | tf_op jit(solution)/shard_map/reduce_scatter | solution.py:270
  449.3 362.3 %reduce-scatter.30.cloned.1.call-start = ((), (), s32[]{:S(2)}) async-start(), calls=%async_computation.8 | async-start | bytes 2654208 | tf_op jit(solution)/shard_map/reduce_scatter | solution.py:271
  458.7 11.3 %copy-start.43 = (bf16[1,166,768]{2,1,0:T(8,128)(2,1)S(1)}, bf16[1,166,768]{2,1,0:T(8,128)(2,1)}, u32[]{:S(2)}) copy-start(bf16[1,166,768]{2,1,0:T(8,128)(2,1)} %get-tuple-element.165) | copy-start | bytes 764932
  813.9 44.1 %copy-start.32 = (f32[3,96,192]{1,2,0:T(8,128)S(1)}, f32[3,96,192]{1,2,0:T(8,128)}, u32[]{:S(2)}) copy-start(f32[3,96,192]{1,2,0:T(8,128)} %copy.108) | copy-start | bytes 663556
  813.9 44.1 %copy-start.33 = (f32[3,96,192]{1,2,0:T(8,128)S(1)}, f32[3,96,192]{1,2,0:T(8,128)}, u32[]{:S(2)}) copy-start(f32[3,96,192]{1,2,0:T(8,128)} %copy.109) | copy-start | bytes 663556
  817.7 43.1 %copy-start.50 = (f32[192,96]{1,0:T(8,128)S(1)}, f32[192,96]{1,0:T(8,128)}, u32[]{:S(2)}) copy-start(f32[192,96]{1,0:T(8,128)} %param.24) | copy-start | bytes 221188
  817.7 43.1 %copy-start.62 = (f32[192,96]{1,0:T(8,128)S(1)}, f32[192,96]{1,0:T(8,128)}, u32[]{:S(2)}) copy-start(f32[192,96]{1,0:T(8,128)} %param.34) | copy-start | bytes 221188
  (76 other events, 301.1 us)
Sparse Core Ops, SparseCore 0:
  10.8 48.2 all-gather.16
  157.7 38.9 all-gather.18
  425.4 60.5 reduce-scatter.35
  489.1 61.4 reduce-scatter.33
  552.1 21.3 all-gather.20
  575.0 22.3 all-gather.22
  601.3 66.8 reduce-scatter.31
  672.2 67.7 reduce-scatter.27
  743.5 67.9 reduce-scatter.29
where the time goes:
time: 880 us; the launch traced here: 874 us
  blocking collectives  325 us (37%)
  waiting for transfers between devices  316 us (36%)
  matrix products  80.6 us (9%)
  local copies, waits for them, and re-layouts  59.6 us (7%)
  other arithmetic  49.9 us (6%)
  between operations  23.1 us (3%)
  starting transfers between devices  19 us (2%)
    unnamed x4, blocking collectives  141 us
    unnamed x20, waiting for transfers between devices  135 us
    reduce_scatter x1, waiting for transfers between devices, body(): lax.psum_scatter(local_sums[3], 'dp', scatter_dimension=1, tiled=True)  69.2 us
    reduce_scatter x1, waiting for transfers between devices, body(): lax.psum_scatter(local_sums[2], 'dp', scatter_dimension=0, tiled=True)  68.6 us
    unnamed x218, local copies, waits for them, and re-layouts  45.4 us
    all_gather x2, waiting for transfers between devices, body(): lax.all_gather(tokens_grad_share, 'mp', axis=0, tiled=True)  43.4 us
    psum x1, blocking collectives, body(): grad_norm = jnp.sqrt(lax.psum(squares, ('dp', 'mp')))  39.4 us
    all_gather x1, blocking collectives, body(): lax.all_gather(inward_weight.astype(jnp.bfloat16), 'dp', axis=1, tiled=True)  38.9 us
  transfers between devices with their start and end apart: 17, of which 7 were waited for; matrix products, arithmetic and copies ran while one was open for 22% of the time, Pallas kernels for 0%

commit v1 on v0

--- a/solution.py
+++ b/solution.py
@@ -1,6 +1,8 @@
 import jax
 import jax.numpy as jnp
 from jax import lax
+from jax.experimental import pallas as pl
+from jax.experimental.pallas import tpu as pltpu
 from jax.sharding import PartitionSpec as P
 
 HEAD_DIM = 64
@@ -345,7 +347,7 @@
     )
 
 
-def solution(mesh):
+def whole_program(mesh, function):
     placed = (
         P("dp", None, None),
         P("dp", None, None),
@@ -368,7 +370,7 @@
         P(None, "dp"),
     )
     return jax.shard_map(
-        body,
+        function,
         mesh=mesh,
         in_specs=placed,
         out_specs=(
@@ -393,3 +395,625 @@
         ),
         check_vma=False,
     )
+
+
+NN = (((1,), (0,)), ((), ()))
+NT = (((1,), (1,)), ((), ()))
+TN = (((0,), (0,)), ((), ()))
+MESH = pl.DeviceIdType.MESH
+F32 = jnp.float32
+BF16 = jnp.bfloat16
+ROWS = 672
+HALF = ROWS // 2
+KEYS = 768
+NEAR_KEYS = 384
+PERIOD = PRIMARY + WRIST + READOUT
+
+
+def dot(left, right, dims=NN):
+    return lax.dot_general(left, right, dims, preferred_element_type=F32)
+
+
+def gelu_both(values):
+    square = values * values
+    inner = 0.7978845608028654 * values * (1.0 + 0.044715 * square)
+    bend = jnp.tanh(inner)
+    half_up = 0.5 + 0.5 * bend
+    slope = half_up + 0.5 * values * (1.0 - bend * bend) * (
+        0.7978845608028654 * (1.0 + 0.134145 * square)
+    )
+    return values * half_up, slope
+
+
+def key_bits(live_steps, has_wrist):
+    place = lax.broadcasted_iota(jnp.int32, (1, KEYS), 1)
+    relative = place - TASK
+    is_task = relative < 0
+    later = relative >= PERIOD
+    offset = jnp.where(later, relative - PERIOD, relative)
+    is_read = offset >= PRIMARY + WRIST
+    is_wrist = jnp.logical_and(offset >= PRIMARY, offset < PRIMARY + WRIST)
+    step_of = jnp.where(later, 1, 0)
+    alive = jnp.logical_and(
+        step_of < live_steps, jnp.logical_or(jnp.logical_not(is_wrist), has_wrist == 1)
+    )
+    bits = jnp.where(is_read, jnp.where(later, 16, 8), jnp.where(later, 4, 2))
+    bits = jnp.where(alive, bits, 0)
+    bits = jnp.where(is_task, 1, bits)
+    return jnp.where(place < SLOTS, bits, 0)
+
+
+def query_bits(first):
+    place = lax.broadcasted_iota(jnp.int32, (HALF, 1), 0) + first
+    relative = place - TASK
+    is_task = relative < 0
+    later = relative >= PERIOD
+    offset = jnp.where(later, relative - PERIOD, relative)
+    is_read = offset >= PRIMARY + WRIST
+    bits = jnp.where(later, 7, 3) + jnp.where(is_read, jnp.where(later, 16, 8), 0)
+    return jnp.where(is_task, 1, bits)
+
+
+class Sems:
+    def __init__(self):
+        self.count = 0
+
+    def take(self):
+        self.count += 1
+        return self.count - 1
+
+
+N_REMOTE = 64
+VMEM_BYTES = 64 * 1024 * 1024 - 65536
+
+
+def fused_kernel(
+    steps, flags, shard_h, tokens_h, back_h, norms,
+    output_h, grad_h, shards_out, table_out,
+    weights, tokens, back, normed_one, queries, keys, values, probs, heads, context,
+    middle, normed_two, hidden, grad_upper, middle_low, out_rows, grad_rows,
+    keep, keep_low, send_a, send_b, ysend_a, ysend_b,
+    recv_attn, recv_low, recv_mid, recv_first,
+    yrecv_attn, yrecv_low, yrecv_mid, yrecv_first,
+    grad_mid, grad_triple, total, x_send, x_recv, z_send, z_recv,
+    table_mine, table_recv,
+    send_sems, recv_sems, local_sems,
+):
+    dp = lax.axis_index("dp")
+    mp = lax.axis_index("mp")
+    z, x = dp // 2, dp % 2
+    y, c = mp // 2, mp % 2
+    core_peer = (dp, y * 2 + 1 - c)
+    y_peer = (dp, (1 - y) * 2 + c)
+    x_peer = (z * 2 + 1 - x, mp)
+    z_peers = [(((z + k) % 4) * 2 + x, mp) for k in (1, 2, 3)]
+    all_peers = [core_peer, y_peer, x_peer] + z_peers
+    far = 1 - y
+    block = weights.shape[1] // 8
+
+    sems = Sems()
+    pending = []
+
+    def send(src, dst, peer):
+        index = sems.take()
+        copy = pltpu.make_async_remote_copy(
+            src_ref=src, dst_ref=dst, send_sem=send_sems.at[index], recv_sem=recv_sems.at[index],
+            device_id=peer, device_id_type=MESH,
+        )
+        copy.start()
+        pending.append(copy)
+        return copy
+
+    def done_sending(copy):
+        copy.wait_send()
+        pending[:] = [other for other in pending if other is not copy]
+
+    def block_rows(index):
+        return pl.ds(pl.multiple_of(index * block, 32), block)
+
+    def half_rows(half):
+        return pl.ds(pl.multiple_of(half * HALF, 16), HALF)
+
+    own_block = block_rows(dp)
+    loads = [
+        pltpu.make_async_copy(shard_h.at[i], weights.at[i, own_block], local_sems.at[i])
+        for i in range(3)
+    ]
+    loads.append(pltpu.make_async_copy(tokens_h, tokens, local_sems.at[3]))
+    loads.append(pltpu.make_async_copy(back_h, back, local_sems.at[4]))
+    for load in loads:
+        load.start()
+
+    barrier = pltpu.get_barrier_semaphore()
+    for peer in all_peers:
+        pl.semaphore_signal(barrier, inc=1, device_id=peer, device_id_type=MESH)
+    pl.semaphore_wait(barrier, len(all_peers))
+
+    z_copies = {}
+    x_copies = {}
+
+    def weights_out(mat):
+        loads[mat].wait()
+        rows = weights.at[mat, own_block]
+        for k in (1, 2, 3):
+            z_copies[mat, k] = send(rows, rows, z_peers[k - 1])
+        x_copies[mat, 0] = send(rows, rows, x_peer)
+
+    def weights_on(mat):
+        for k in (1, 3, 2):
+            z_copies[mat, k].wait_recv()
+            rows = weights.at[mat, block_rows(((z + 4 - k) % 4) * 2 + x)]
+            x_copies[mat, k] = send(rows, rows, x_peer)
+
+    def weights_in(mat):
+        for k in (0, 1, 3, 2):
+            x_copies[mat, k].wait_recv()
+
+    def norm_stats(rows):
+        centre = rows - jnp.mean(rows, axis=-1, keepdims=True)
+        inverse = lax.rsqrt(jnp.mean(centre * centre, axis=-1, keepdims=True) + NORM_EPSILON)
+        return centre * inverse, inverse
+
+    def norm_back(grad_result, normal, inverse, gain_row):
+        scaled = grad_result * gain_row
+        return inverse * (
+            scaled
+            - jnp.mean(scaled, axis=-1, keepdims=True)
+            - normal * jnp.mean(scaled * normal, axis=-1, keepdims=True)
+        )
+
+    def first_norm(item):
+        @pl.loop(0, ROWS // 112)
+        def _(index):
+            rows = pl.ds(pl.multiple_of(index * 112, 16), 112)
+            normal, _ = norm_stats(tokens[item, rows, :].astype(F32))
+            normed_one[item, rows, :] = (normal * norms[0:1, :] + norms[1:2, :]).astype(BF16)
+
+    weights_out(0)
+    loads[3].wait()
+    first_norm(far)
+    weights_on(0)
+    weights_out(1)
+    weights_out(2)
+    first_norm(y)
+    loads[4].wait()
+    zero_rows = jnp.zeros((KEYS - ROWS, HEAD_DIM), BF16)
+    for i in range(6):
+        keys[i, ROWS:KEYS, :] = zero_rows
+        values[i, ROWS:KEYS, :] = zero_rows
+    weights_in(0)
+
+    def project(item):
+        @pl.loop(0, 2)
+        def _(half):
+            rows = half_rows(half)
+            joined = dot(normed_one[item, rows, :], weights[0, :, 0:576])
+            for head in range(3):
+                low = head * HEAD_DIM
+                queries[item * 3 + head, rows, :] = (
+                    joined[:, low : low + HEAD_DIM].astype(BF16) * HEAD_DIM ** (-0.5)
+                ).astype(BF16)
+                low += 192
+                keys[item * 3 + head, rows, :] = joined[:, low : low + HEAD_DIM].astype(BF16)
+                low += 192
+                values[item * 3 + head, rows, :] = joined[:, low : low + HEAD_DIM].astype(BF16)
+
+    def attend(item):
+        bits = key_bits(steps[item], flags[item])
+
+        @pl.loop(0, 3)
+        def _(head):
+            at = item * 3 + head
+            for half, extent in ((0, NEAR_KEYS), (1, KEYS)):
+                first = half * HALF
+                scores = dot(queries[at, first : first + HALF, :], keys[at, 0:extent, :], NT)
+                seen = jnp.bitwise_and(bits[:, 0:extent], query_bits(first)) != 0
+                scores = jnp.where(seen, scores, NEGATIVE)
+                spread = jnp.exp(scores - jnp.max(scores, axis=-1, keepdims=True))
+                scale = 1.0 / jnp.sum(spread, axis=-1, keepdims=True)
+                low = (spread * scale).astype(BF16)
+                probs[at, first : first + HALF, 0:extent] = low
+                heads[at, first : first + HALF, :] = dot(low, values[at, 0:extent, :]).astype(BF16)
+
+    def join_heads(source, item, half):
+        rows = half_rows(half)
+        return jnp.concatenate([source[item * 3 + head, rows, :] for head in range(3)], axis=1)
+
+    def attention_out(item, slot):
+        for half in (0, 1):
+            context[item, half * HALF : (half + 1) * HALF, :] = join_heads(heads, item, half)
+        outward = weights[0, :, 576:768]
+        send_a[slot] = dot(context[item, half_rows(1 - c), :], outward, NT).astype(BF16)
+        copy = send(send_a.at[slot], recv_attn.at[slot], core_peer)
+        keep[slot] = dot(context[item, half_rows(c), :], outward, NT)
+        return copy
+
+    project(far)
+    attend(far)
+    attn_far = attention_out(far, 0)
+    project(y)
+    attn_far.wait_recv()
+    ysend_a[...] = (keep[0] + recv_attn[0].astype(F32)).astype(BF16)
+    attn_y = send(ysend_a, yrecv_attn, y_peer)
+    weights_on(1)
+    attend(y)
+    weights_on(2)
+    attn_near = attention_out(y, 1)
+    attn_near.wait_recv()
+    attn_y.wait_recv()
+    mine = half_rows(c)
+    middle[...] = (
+        tokens[y, mine, :].astype(F32)
+        + keep[1]
+        + recv_attn[1].astype(F32)
+        + yrecv_attn[...].astype(F32)
+    )
+    normal_two, _ = norm_stats(middle[...])
+    normed_two[y, mine, :] = (normal_two * norms[2:3, :] + norms[3:4, :]).astype(BF16)
+
+    def share_rows(buffer):
+        rows = buffer.at[y, mine]
+        return send(rows, rows, core_peer), send(rows, rows, y_peer)
+
+    def pass_on(buffer, copy):
+        copy.wait_recv()
+        rows = buffer.at[far, mine]
+        return send(rows, rows, core_peer)
+
+    two_core, two_y = share_rows(normed_two)
+    weights_in(1)
+    weights_in(2)
+    done_sending(attn_far)
+    done_sending(attn_near)
+    done_sending(attn_y)
+
+    def feed_forward(item, half, keep_slot, send_slot):
+        rows = half_rows(half)
+        upper = dot(normed_two[item, rows, :], weights[1])
+        grown, slope = gelu_both(upper)
+        grown = grown.astype(BF16)
+        hidden[item, rows, :] = grown
+        pull = (dot(back[item, rows, :], weights[2]) * slope).astype(BF16)
+        grad_upper[item, rows, :] = pull
+        terms = dot(pull, weights[1], NT)
+        lowered = dot(grown, weights[2], NT)
+        if keep_slot is not None:
+            keep[keep_slot] = terms
+            keep_low[keep_slot] = lowered
+            return None
+        send_a[send_slot] = terms.astype(BF16)
+        first = send(send_a.at[send_slot], recv_mid.at[send_slot], core_peer)
+        send_b[send_slot] = lowered.astype(BF16)
+        return first, send(send_b.at[send_slot], recv_low.at[send_slot], core_peer)
+
+    feed_forward(y, c, 1, None)
+    two_core.wait_recv()
+    mid_near, low_near = feed_forward(y, 1 - c, None, 1)
+    two_on = pass_on(normed_two, two_y)
+    feed_forward(far, c, 0, None)
+    two_on.wait_recv()
+    mid_far, low_far = feed_forward(far, 1 - c, None, 0)
+    mid_far.wait_recv()
+    ysend_a[...] = (keep[0] + recv_mid[0].astype(F32)).astype(BF16)
+    mid_y = send(ysend_a, yrecv_mid, y_peer)
+    low_far.wait_recv()
+    ysend_b[...] = (keep_low[0] + recv_low[0].astype(F32)).astype(BF16)
+    low_y = send(ysend_b, yrecv_low, y_peer)
+
+    def band_grad(slot, first, width, left_of, right_of):
+        total[slot, :, first : first + width] = dot(left_of(0), right_of(0), TN) + dot(
+            left_of(1), right_of(1), TN
+        )
+
+    def grads_out(mat, slot):
+        for k in range(4):
+            x_send[mat, k] = total[slot, block_rows(2 * k + 1 - x), :].astype(BF16)
+        return send(x_send.at[mat], x_recv.at[mat], x_peer)
+
+    def grads_on(mat, slot, copy):
+        copy.wait_recv()
+        sent = []
+        for k in (2, 1, 3):
+            other = (z + k) % 4
+            z_send[mat, k - 1] = (
+                total[slot, block_rows(2 * other + x), :] + x_recv[mat, other].astype(F32)
+            ).astype(BF16)
+            sent.append(send(z_send.at[mat, k - 1], z_recv.at[mat, k - 1], z_peers[k - 1]))
+        shards_out[mat] = total[slot, own_block, :] + x_recv[mat, z].astype(F32)
+        return sent
+
+    def grads_in(mat, sent):
+        for copy in sent:
+            copy.wait_recv()
+        summed = shards_out[mat]
+        for k in range(3):
+            summed += z_recv[mat, k].astype(F32)
+        shards_out[mat] = summed
+        return jnp.sum(summed * summed)
+
+    for first in (0, 256, 512):
+        band_grad(
+            0, first, 256,
+            lambda i: back[i], lambda i, f=first: hidden[i, :, f : f + 256],
+        )
+    down_x = grads_out(2, 0)
+    for first in (0, 256, 512):
+        band_grad(
+            1, first, 256,
+            lambda i: normed_two[i], lambda i, f=first: grad_upper[i, :, f : f + 256],
+        )
+    up_x = grads_out(1, 1)
+
+    mid_near.wait_recv()
+    mid_y.wait_recv()
+    grad_two = keep[1] + recv_mid[1].astype(F32) + yrecv_mid[...].astype(F32)
+    normal_two, inverse_two = norm_stats(middle[...])
+    table_mine[2:3, :] = jnp.sum(grad_two * normal_two, axis=0, keepdims=True)
+    table_mine[3:4, :] = jnp.sum(grad_two, axis=0, keepdims=True)
+    grad_mid[...] = back[y, mine, :].astype(F32) + norm_back(
+        grad_two, normal_two, inverse_two, norms[2:3, :]
+    )
+    middle_low[y, mine, :] = grad_mid[...].astype(BF16)
+    ml_core, ml_y = share_rows(middle_low)
+
+    low_near.wait_recv()
+    low_y.wait_recv()
+    out_rows[y, mine, :] = (
+        middle[...] + keep_low[1] + recv_low[1].astype(F32) + yrecv_low[...].astype(F32)
+    ).astype(BF16)
+    out_core, out_y = share_rows(out_rows)
+    done_sending(mid_near)
+    done_sending(mid_far)
+    done_sending(mid_y)
+    down_z = grads_on(2, 0, down_x)
+
+    def attend_back(item):
+        for half in (0, 1):
+            rows = half_rows(half)
+            pulled = dot(middle_low[item, rows, :], weights[0, :, 576:768]).astype(BF16)
+            for head in range(3):
+                heads[item * 3 + head, rows, :] = pulled[:, head * HEAD_DIM : (head + 1) * HEAD_DIM]
+
+        @pl.loop(0, 3)
+        def _(head):
+            at = item * 3 + head
+            grad_key = None
+            grad_value = None
+            key_rows = keys[at]
+            value_rows = values[at]
+            for half, extent in ((1, KEYS), (0, NEAR_KEYS)):
+                first = half * HALF
+                rows = slice(first, first + HALF)
+                pulled = heads[at, rows, :]
+                weight = dot(pulled, value_rows[0:extent], NT)
+                low = probs[at, rows, 0:extent]
+                wide = low.astype(F32)
+                weight = wide * weight
+                moved = (weight - wide * jnp.sum(weight, axis=-1, keepdims=True)).astype(BF16)
+                asked = queries[at, rows, :]
+                part_key = dot(moved, asked, TN)
+                part_value = dot(low, pulled, TN)
+                queries[at, rows, :] = (
+                    dot(moved, key_rows[0:extent]) * HEAD_DIM ** (-0.5)
+                ).astype(BF16)
+                if grad_key is None:
+                    grad_key, grad_value = part_key, part_value
+                else:
+                    keys[at, 0:extent, :] = (grad_key[0:extent] + part_key).astype(BF16)
+                    values[at, 0:extent, :] = (grad_value[0:extent] + part_value).astype(BF16)
+                    keys[at, extent:KEYS, :] = grad_key[extent:KEYS].astype(BF16)
+                    values[at, extent:KEYS, :] = grad_value[extent:KEYS].astype(BF16)
+
+        for half in (0, 1):
+            rows = slice(half * HALF, (half + 1) * HALF)
+            grad_triple[item, rows, :] = jnp.concatenate(
+                [
+                    source[item * 3 + head, rows, :]
+                    for source in (queries, keys, values)
+                    for head in range(3)
+                ],
+                axis=1,
+            )
+
+    def first_terms(item, slot):
+        inward = weights[0, :, 0:576]
+        send_a[slot] = dot(grad_triple[item, half_rows(1 - c), :], inward, NT).astype(BF16)
+        copy = send(send_a.at[slot], recv_first.at[slot], core_peer)
+        keep[slot] = dot(grad_triple[item, half_rows(c), :], inward, NT)
+        return copy
+
+    ml_on = pass_on(middle_low, ml_y)
+    ml_on.wait_recv()
+    attend_back(far)
+    first_far = first_terms(far, 0)
+    up_z = grads_on(1, 1, up_x)
+    out_on = pass_on(out_rows, out_y)
+    first_far.wait_recv()
+    ysend_a[...] = (keep[0] + recv_first[0].astype(F32)).astype(BF16)
+    first_y = send(ysend_a, yrecv_first, y_peer)
+    ml_core.wait_recv()
+    attend_back(y)
+    first_near = first_terms(y, 1)
+    for first, width in ((0, 256), (256, 256), (512, 64)):
+        band_grad(
+            0, first, width,
+            lambda i: normed_one[i], lambda i, f=first, w=width: grad_triple[i, :, f : f + w],
+        )
+    band_grad(0, 576, 192, lambda i: middle_low[i], lambda i: context[i])
+    in_x = grads_out(0, 0)
+
+    first_near.wait_recv()
+    first_y.wait_recv()
+    grad_one = keep[1] + recv_first[1].astype(F32) + yrecv_first[...].astype(F32)
+    normal_one, inverse_one = norm_stats(tokens[y, mine, :].astype(F32))
+    table_mine[0:1, :] = jnp.sum(grad_one * normal_one, axis=0, keepdims=True)
+    table_mine[1:2, :] = jnp.sum(grad_one, axis=0, keepdims=True)
+    grad_rows[y, mine, :] = (
+        grad_mid[...] + norm_back(grad_one, normal_one, inverse_one, norms[0:1, :])
+    ).astype(BF16)
+    rows_core, rows_y = share_rows(grad_rows)
+
+    out_core.wait_recv()
+    out_on.wait_recv()
+    store_out = pltpu.make_async_copy(out_rows, output_h, local_sems.at[5])
+    store_out.start()
+    in_z = grads_on(0, 0, in_x)
+    squares = grads_in(2, down_z) + grads_in(1, up_z)
+    rows_on = pass_on(grad_rows, rows_y)
+    squares += grads_in(0, in_z)
+    table_mine[4:8, :] = jnp.broadcast_to(squares, (4, table_mine.shape[1]))
+
+    rows_core.wait_recv()
+    rows_on.wait_recv()
+    store_rows = pltpu.make_async_copy(grad_rows, grad_h, local_sems.at[6])
+    store_rows.start()
+
+    at_hop = 0
+    for peer in (core_peer, y_peer, x_peer):
+        hop = send(table_mine, table_recv.at[at_hop], peer)
+        hop.wait_recv()
+        done_sending(hop)
+        table_mine[...] = table_mine[...] + table_recv[at_hop]
+        at_hop += 1
+    hops = []
+    for k in (1, 2, 3):
+        hops.append(send(table_mine, table_recv.at[2 + k], z_peers[k - 1]))
+    for hop in hops:
+        hop.wait_recv()
+    parts = [table_mine[...], table_recv[3], table_recv[4], table_recv[5]]
+    ordered = None
+    for level in range(4):
+        piece = parts[0]
+        for k in (1, 2, 3):
+            piece = jnp.where((level + k) % 4 == z, parts[k], piece)
+        ordered = piece if ordered is None else ordered + piece
+    table_out[...] = ordered
+
+    store_out.wait()
+    store_rows.wait()
+    for copy in list(pending):
+        copy.wait_send()
+
+
+def fused_body(
+    tokens, cotangent, step_counts, wrist_flags,
+    inward_weight, outward_weight, upward_weight, downward_weight, norm_table,
+    momentum_inward, momentum_outward, momentum_upward, momentum_downward, momentum_norms,
+    variance_inward, variance_outward, variance_upward, variance_downward, variance_norms,
+):
+    width = norm_table.shape[1]
+    block = upward_weight.shape[0]
+    shard = jnp.stack(
+        [
+            jnp.concatenate(
+                [inward_weight[0], inward_weight[1], inward_weight[2], outward_weight.T], axis=1
+            ),
+            upward_weight,
+            downward_weight.T,
+        ]
+    ).astype(BF16)
+    padding = ((0, 0), (0, ROWS - SLOTS), (0, 0))
+    any_spec = pl.BlockSpec(memory_space=pl.ANY)
+    vmem = pl.BlockSpec(memory_space=pltpu.VMEM)
+    smem = pl.BlockSpec(memory_space=pltpu.SMEM)
+    rows = pltpu.VMEM((2, ROWS, width), BF16)
+    halves = pltpu.VMEM((2, HALF, width), BF16)
+    half = pltpu.VMEM((HALF, width), BF16)
+    keep = pltpu.VMEM((2, HALF, width), F32)
+    output, grads, shards, table = pl.pallas_call(
+        fused_kernel,
+        out_shape=(
+            jax.ShapeDtypeStruct((2, ROWS, width), BF16),
+            jax.ShapeDtypeStruct((2, ROWS, width), BF16),
+            jax.ShapeDtypeStruct((3, block, width), F32),
+            jax.ShapeDtypeStruct((8, width), F32),
+        ),
+        in_specs=[smem, smem, any_spec, any_spec, any_spec, vmem],
+        out_specs=(any_spec, any_spec, vmem, vmem),
+        scratch_shapes=[
+            pltpu.VMEM((3, width, width), BF16),
+            rows,
+            rows,
+            rows,
+            pltpu.VMEM((6, ROWS, HEAD_DIM), BF16),
+            pltpu.VMEM((6, KEYS, HEAD_DIM), BF16),
+            pltpu.VMEM((6, KEYS, HEAD_DIM), BF16),
+            pltpu.VMEM((6, ROWS, KEYS), BF16),
+            pltpu.VMEM((6, ROWS, HEAD_DIM), BF16),
+            pltpu.VMEM((2, ROWS, 192), BF16),
+            pltpu.VMEM((HALF, width), F32),
+            rows,
+            rows,
+            rows,
+            rows,
+            rows,
+            rows,
+            keep,
+            keep,
+            halves,
+            halves,
+            half,
+            half,
+            halves,
+            halves,
+            halves,
+            halves,
+            half,
+            half,
+            half,
+            half,
+            pltpu.VMEM((HALF, width), F32),
+            pltpu.VMEM((2, ROWS, 576), BF16),
+            pltpu.VMEM((2, width, width), F32),
+            pltpu.VMEM((3, 4, block, width), BF16),
+            pltpu.VMEM((3, 4, block, width), BF16),
+            pltpu.VMEM((3, 3, block, width), BF16),
+            pltpu.VMEM((3, 3, block, width), BF16),
+            pltpu.VMEM((8, width), F32),
+            pltpu.VMEM((6, 8, width), F32),
+            pltpu.SemaphoreType.DMA((N_REMOTE,)),
+            pltpu.SemaphoreType.DMA((N_REMOTE,)),
+            pltpu.SemaphoreType.DMA((7,)),
+        ],
+        compiler_params=pltpu.CompilerParams(
+            collective_id=0, has_side_effects=True, vmem_limit_bytes=VMEM_BYTES
+        ),
+        name="block_step",
+    )(
+        step_counts,
+        wrist_flags,
+        shard,
+        jnp.pad(tokens, padding),
+        jnp.pad(cotangent, padding),
+        norm_table,
+    )
+    part = inward_weight.shape[2]
+    grad_inward = jnp.stack([shards[0, :, i * part : (i + 1) * part] for i in range(3)])
+    grad_outward = shards[0, :, 3 * part :].T
+    table_sums = table[:4]
+    grad_norm = jnp.sqrt(table[4, 0] + jnp.sum(table_sums * table_sums))
+    clip_scale = jnp.minimum(1.0, CLIP_NORM / (grad_norm + 1e-06))
+    shard_width = momentum_norms.shape[1]
+    start = lax.axis_index("dp") * shard_width
+    own_table = lax.dynamic_slice_in_dim(norm_table, start, shard_width, 1)
+    own_sums = lax.dynamic_slice_in_dim(table_sums, start, shard_width, 1)
+    updated = []
+    for master, momentum, variance, gradient, rate, decay in (
+        (inward_weight, momentum_inward, variance_inward, grad_inward, RATE_INWARD, WEIGHT_DECAY),
+        (outward_weight, momentum_outward, variance_outward, grad_outward, RATE_OUTWARD, WEIGHT_DECAY),
+        (upward_weight, momentum_upward, variance_upward, shards[1], RATE_UPWARD, WEIGHT_DECAY),
+        (downward_weight, momentum_downward, variance_downward, shards[2].T, RATE_DOWNWARD, WEIGHT_DECAY),
+        (own_table, momentum_norms, variance_norms, own_sums, RATE_NORMS, 0.0),
+    ):
+        updated.extend(adam_update(master, momentum, variance, gradient, clip_scale, rate, decay))
+    return (
+        output[:, :SLOTS],
+        grads[:, :SLOTS].astype(F32),
+        grad_norm,
+        *updated,
+    )
+
+
+def solution(mesh):
+    fits = mesh.shape["dp"] == 8 and mesh.shape["mp"] == 4
+    return whole_program(mesh, fused_body if fits else body)

time: 880 us -> 191 us (0.22)
  blocking collectives: 325 us -> 0 us
  waiting for transfers between devices: 316 us -> 0 us
  Pallas kernels: 0 us -> 164 us
  matrix products: 80.6 us -> 0 us
  local copies, waits for them, and re-layouts: 59.6 us -> 11 us
  other arithmetic: 49.9 us -> 11.6 us
  between operations: 23.1 us -> 3.39 us
  starting transfers between devices: 19 us -> 0 us
    pallas_call x0 -> x1, Pallas kernels: none -> 164 us  [fused_body(): pl.pallas_call(fused_kernel, out_shape=(jax.ShapeDtypeStruct((2, ROWS, wi...]
    all_gather x10 -> x0, blocking collectives: 145 us -> none  [the longest x1 38.9 us: body(): lax.all_gather(inward_weight.astype(jnp.bfloat16), 'dp', axis=1, tiled=True)]
    unnamed x4 -> x0, blocking collectives: 141 us -> none
    reduce_scatter x2 -> x0, waiting for transfers between devices: 138 us -> none  [the longest x1 69.2 us: body(): lax.psum_scatter(local_sums[3], 'dp', scatter_dimension=1, tiled=True)]
    unnamed x20 -> x0, waiting for transfers between devices: 135 us -> none
    dot_general x34 -> x0, matrix products: 78.4 us -> none  [the longest x2 9.87 us: body(): jnp.einsum('nhqk,nqhd->nkhd', attention_again, grad_context, preferred_el...]
    all_gather x4 -> x0, waiting for transfers between devices: 43.4 us -> none  [the longest x2 43.4 us: body(): lax.all_gather(tokens_grad_share, 'mp', axis=0, tiled=True)]
    unnamed x218 -> x46, local copies, waits for them, and re-layouts: 45.4 us -> 4.34 us
  transfers between devices with their start and end apart: 17 -> 0, of which waited for: 7 -> 0; matrix products, arithmetic and copies ran while one was open for 22% -> 0% of each run, Pallas kernels for 0% -> 0%
where the time goes in v1:
time: 191 us; the launch traced here: 190 us
  Pallas kernels  164 us (86%)
  other arithmetic  11.6 us (6%)
  local copies, waits for them, and re-layouts  11 us (6%)
  between operations  3.39 us (2%)
    pallas_call x1, Pallas kernels, fused_body(): pl.pallas_call(fused_kernel, out_shape=(jax.ShapeDtypeStruct((2, ROWS, wi...  164 us
    sub x5, other arithmetic, adam_update(): master - step_rate * (first_hat / (jnp.sqrt(second_hat) + ADAM_EPSILON) +...  4.68 us
    unnamed x46, local copies, waits for them, and re-layouts  4.34 us

profile of v1, /device:TPU:0, one launch (start us, length us, event | category | flops | bytes accessed | tf_op | source)
XLA Modules:
  0.0 190.3 jit_solution(11094696163819061076)
XLA Ops:
  0.7 1.1 convert_bitcast_fusion
  1.8 1.0 convert_bitcast_fusion.1
  2.8 1.0 copy.37
  3.8 0.0 copy-start.7
  3.8 1.0 convert.26
  4.8 0.1 maximum_bitcast_fusion
  4.9 0.8 pad_maximum_fusion.shard_h
  5.8 1.4 pad.7.tokens_h
  7.2 0.9 copy-done.1
  8.1 1.5 pad.8.back_h
  9.5 164.3 %block_step.1 = (bf16[2,672,768]{2,1,0:T(8,128)(2,1)}, bf16[2,672,768]{2,1,0:T(8,128)(2,1)}, f32[3,96,768]{2,1,0:T(8,128)}, f32[8,768]{1,0:T(8,128)}) custom-call(s32[2]{0:T(128)} %steps.1, s32[2]{0:T(128)} %flags.1, bf16[3,96,768]{2,1,0:T(8,128)(2,1)} %pad_maximum_fusion.shard_h, bf16[2,672,768]{2,1,0:T(8,128)(2,1)} %pad.7.tokens_h, ...), custom_call_target="tpu_custom_call" | custom-call | tf_op jit(solution)/shard_map/block_step/pallas_call | solution.py:923
  173.8 3.1 %slice.45 = bf16[2,664,768]{2,1,0:T(8,128)(2,1)} slice(bf16[2,672,768]{2,1,0:T(8,128)(2,1)} %get-tuple-element.22), slice={[0:2], [0:664], [0:768]} | slice | bytes 4079616 | tf_op jit(solution)/shard_map/slice | solution.py:1010
  177.0 0.0 copy-start.9
  177.0 0.0 copy-start.10
  177.0 2.3 %slice_convert_fusion = f32[2,664,768]{2,1,0:T(8,128)} fusion(bf16[2,672,768]{2,1,0:T(8,128)(2,1)S(1)} %copy-done.2), kind=kLoop, calls=%fused_computation | loop fusion | flops 1019904 | bytes 6119424 | tf_op jit(solution)/shard_map/convert_element_type | solution.py:1011
  179.3 0.5 slice.47
  179.8 0.6 fusion.17
  181.8 0.0 copy-start.4
  181.8 0.0 copy-start.11
  181.8 0.0 copy-start.12
  181.8 0.1 fusion.16
  182.0 1.1 multiply_subtract_fusion.2
  183.0 0.1 copy.39
  183.1 0.1 copy.38
  183.2 0.2 multiply_subtract_fusion.3
  183.4 0.7 copy.42
  184.1 0.7 copy.43
  184.9 0.7 copy.44
  185.6 0.0 copy-start.19
  185.6 1.1 multiply_subtract_fusion.1
  186.7 1.1 multiply_subtract_fusion
  187.8 1.4 multiply_subtract_fusion.4
  (34 shorter events, 0.1 us)
Async XLA Ops:
  0.7 5.1 %copy-start = (bf16[2,664,768]{2,1,0:T(8,128)(2,1)S(1)}, bf16[2,664,768]{2,1,0:T(8,128)(2,1)}, u32[]{:S(2)}) copy-start(bf16[2,664,768]{2,1,0:T(8,128)(2,1)} %param.19) | copy-start | bytes 6119428
  3.8 3.4 %copy-start.7 = (f32[192,96]{0,1:T(8,128)}, f32[192,96]{0,1:T(8,128)S(1)}, u32[]{:S(2)}) copy-start(f32[192,96]{0,1:T(8,128)S(1)} %copy.37) | copy-start | bytes 221188
  5.8 2.3 %copy-start.1 = (bf16[2,664,768]{2,1,0:T(8,128)(2,1)S(1)}, bf16[2,664,768]{2,1,0:T(8,128)(2,1)}, u32[]{:S(2)}) copy-start(bf16[2,664,768]{2,1,0:T(8,128)(2,1)} %param.20) | copy-start | bytes 6119428
  173.8 3.2 %copy-start.2 = (bf16[2,672,768]{2,1,0:T(8,128)(2,1)S(1)}, bf16[2,672,768]{2,1,0:T(8,128)(2,1)}, u32[]{:S(2)}) copy-start(bf16[2,672,768]{2,1,0:T(8,128)(2,1)} %get-tuple-element.23) | copy-start | bytes 6193156
  177.0 2.3 %copy-start.17 = (f32[8,768]{1,0:T(8,128)S(1)}, f32[8,768]{1,0:T(8,128)}, u32[]{:S(2)}) copy-start(f32[8,768]{1,0:T(8,128)} %get-tuple-element.24) | copy-start | bytes 73732
  177.0 4.8 %copy-start.6 = (f32[3,96,768]{2,1,0:T(8,128)S(1)}, f32[3,96,768]{2,1,0:T(8,128)}, u32[]{:S(2)}) copy-start(f32[3,96,768]{2,1,0:T(8,128)} %get-tuple-element.25) | copy-start | bytes 2654212
  177.0 4.9 %copy-start.3 = (f32[3,96,192]{2,1,0:T(8,128)S(1)}, f32[3,96,192]{2,1,0:T(8,128)}, u32[]{:S(2)}) copy-start(f32[3,96,192]{2,1,0:T(8,128)} %param.23) | copy-start | bytes 663556
  177.0 4.9 %copy-start.9 = (f32[3,96,192]{2,1,0:T(8,128)S(1)}, f32[3,96,192]{2,1,0:T(8,128)}, u32[]{:S(2)}) copy-start(f32[3,96,192]{2,1,0:T(8,128)} %param.33) | copy-start | bytes 663556
  177.0 4.9 %copy-start.10 = (f32[3,96,192]{2,1,0:T(8,128)S(1)}, f32[3,96,192]{2,1,0:T(8,128)}, u32[]{:S(2)}) copy-start(f32[3,96,192]{2,1,0:T(8,128)} %param.28) | copy-start | bytes 663556
  179.3 3.7 %copy-start.15 = (f32[192,96]{1,0:T(8,128)S(1)}, f32[192,96]{1,0:T(8,128)}, u32[]{:S(2)}) copy-start(f32[192,96]{1,0:T(8,128)} %param.34) | copy-start | bytes 221188
  179.3 3.8 %copy-start.16 = (f32[192,96]{1,0:T(8,128)S(1)}, f32[192,96]{1,0:T(8,128)}, u32[]{:S(2)}) copy-start(f32[192,96]{1,0:T(8,128)} %param.29) | copy-start | bytes 221188
  179.3 3.9 %copy-start.8 = (f32[192,96]{0,1:T(8,128)S(1)}, f32[192,96]{0,1:T(8,128)}, u32[]{:S(2)}) copy-start(f32[192,96]{0,1:T(8,128)} %copy-done.7) | copy-start | bytes 221188
  181.8 3.8 %copy-start.4 = (f32[96,768]{1,0:T(8,128)S(1)}, f32[96,768]{1,0:T(8,128)}, u32[]{:S(2)}) copy-start(f32[96,768]{1,0:T(8,128)} %param.25) | copy-start | bytes 884740
  181.8 3.8 %copy-start.11 = (f32[96,768]{1,0:T(8,128)S(1)}, f32[96,768]{1,0:T(8,128)}, u32[]{:S(2)}) copy-start(f32[96,768]{1,0:T(8,128)} %param.35) | copy-start | bytes 884740
  181.8 3.8 %copy-start.12 = (f32[96,768]{1,0:T(8,128)S(1)}, f32[96,768]{1,0:T(8,128)}, u32[]{:S(2)}) copy-start(f32[96,768]{1,0:T(8,128)} %param.30) | copy-start | bytes 884740
  183.0 3.7 %copy-start.5 = (f32[768,96]{0,1:T(8,128)S(1)}, f32[768,96]{0,1:T(8,128)}, u32[]{:S(2)}) copy-start(f32[768,96]{0,1:T(8,128)} %param.26) | copy-start | bytes 884740
  183.0 3.7 %copy-start.13 = (f32[768,96]{0,1:T(8,128)S(1)}, f32[768,96]{0,1:T(8,128)}, u32[]{:S(2)}) copy-start(f32[768,96]{0,1:T(8,128)} %param.36) | copy-start | bytes 884740
  183.0 3.7 %copy-start.14 = (f32[768,96]{0,1:T(8,128)S(1)}, f32[768,96]{0,1:T(8,128)}, u32[]{:S(2)}) copy-start(f32[768,96]{0,1:T(8,128)} %param.31) | copy-start | bytes 884740
  185.6 2.1 %copy-start.18 = (f32[4,96]{1,0:T(4,128)S(1)}, f32[4,96]{1,0:T(4,128)}, u32[]{:S(2)}) copy-start(f32[4,96]{1,0:T(4,128)} %param.37) | copy-start | bytes 4612
  185.6 2.1 %copy-start.19 = (f32[4,96]{1,0:T(4,128)S(1)}, f32[4,96]{1,0:T(4,128)}, u32[]{:S(2)}) copy-start(f32[4,96]{1,0:T(4,128)} %param.32) | copy-start | bytes 4612

commit v2 on v1

--- a/solution.py
+++ b/solution.py
@@ -454,16 +454,7 @@
     return jnp.where(is_task, 1, bits)
 
 
-class Sems:
-    def __init__(self):
-        self.count = 0
-
-    def take(self):
-        self.count += 1
-        return self.count - 1
-
-
-N_REMOTE = 64
+N_REMOTE = 128
 VMEM_BYTES = 64 * 1024 * 1024 - 65536
 
 
@@ -471,10 +462,9 @@
     steps, flags, shard_h, tokens_h, back_h, norms,
     output_h, grad_h, shards_out, table_out,
     weights, tokens, back, normed_one, queries, keys, values, probs, heads, context,
-    middle, normed_two, hidden, grad_upper, middle_low, out_rows, grad_rows,
-    keep, keep_low, send_a, send_b, ysend_a, ysend_b,
-    recv_attn, recv_low, recv_mid, recv_first,
-    yrecv_attn, yrecv_low, yrecv_mid, yrecv_first,
+    middle, normed_two, hidden, grad_upper, middle_low, out_half, grad_half,
+    keep, keep_low, send_a, send_b,
+    recv_one, recv_mid, recv_low, swapped_one, swapped_mid, swapped_low,
     grad_mid, grad_triple, total, x_send, x_recv, z_send, z_recv,
     table_mine, table_recv,
     send_sems, recv_sems, local_sems,
@@ -488,25 +478,27 @@
     x_peer = (z * 2 + 1 - x, mp)
     z_peers = [(((z + k) % 4) * 2 + x, mp) for k in (1, 2, 3)]
     all_peers = [core_peer, y_peer, x_peer] + z_peers
-    far = 1 - y
     block = weights.shape[1] // 8
-
-    sems = Sems()
+    used = []
     pending = []
 
-    def send(src, dst, peer):
-        index = sems.take()
-        copy = pltpu.make_async_remote_copy(
+    def describe(index, src, dst, peer):
+        return pltpu.make_async_remote_copy(
             src_ref=src, dst_ref=dst, send_sem=send_sems.at[index], recv_sem=recv_sems.at[index],
             device_id=peer, device_id_type=MESH,
         )
+
+    def send(src, dst, peer):
+        used.append(0)
+        copy = describe(len(used) - 1, src, dst, peer)
         copy.start()
         pending.append(copy)
         return copy
 
-    def done_sending(copy):
-        copy.wait_send()
-        pending[:] = [other for other in pending if other is not copy]
+    def done_sending(*copies):
+        for copy in copies:
+            copy.wait_send()
+            pending[:] = [other for other in pending if other is not copy]
 
     def block_rows(index):
         return pl.ds(pl.multiple_of(index * block, 32), block)
@@ -514,6 +506,7 @@
     def half_rows(half):
         return pl.ds(pl.multiple_of(half * HALF, 16), HALF)
 
+    mine = half_rows(c)
     own_block = block_rows(dp)
     loads = [
         pltpu.make_async_copy(shard_h.at[i], weights.at[i, own_block], local_sems.at[i])
@@ -529,25 +522,73 @@
         pl.semaphore_signal(barrier, inc=1, device_id=peer, device_id_type=MESH)
     pl.semaphore_wait(barrier, len(all_peers))
 
-    z_copies = {}
-    x_copies = {}
+    later = []
+    z_index = {}
+    for mat in range(3):
+        for sign in (1, -1):
+            for j in (1, 2, 3):
+                z_index[mat, sign, j] = len(used)
+                used.append(0)
+                z_index[mat, sign, j, "x"] = len(used)
+                used.append(0)
+    own_x = {}
+
+    def z_send_block(mat, sign, j):
+        origin = z - sign * (j - 1)
+        rows = weights.at[mat, block_rows(origin * 2 + x)]
+        there = ((z + sign) * 2 + x, mp)
+        copy = describe(z_index[mat, sign, j], rows, rows, there)
+        wanted = jnp.logical_and(
+            jnp.logical_and(origin >= 0, origin <= 3), z < 3 if sign == 1 else z > 0
+        )
+
+        @pl.when(wanted)
+        def _():
+            copy.start()
+
+        later.append((wanted, copy))
 
     def weights_out(mat):
         loads[mat].wait()
+        for sign in (1, -1):
+            z_send_block(mat, sign, 1)
         rows = weights.at[mat, own_block]
-        for k in (1, 2, 3):
-            z_copies[mat, k] = send(rows, rows, z_peers[k - 1])
-        x_copies[mat, 0] = send(rows, rows, x_peer)
-
-    def weights_on(mat):
-        for k in (1, 3, 2):
-            z_copies[mat, k].wait_recv()
-            rows = weights.at[mat, block_rows(((z + 4 - k) % 4) * 2 + x)]
-            x_copies[mat, k] = send(rows, rows, x_peer)
+        own_x[mat] = send(rows, rows, x_peer)
+
+    def arrives(sign, j):
+        return z >= j if sign == 1 else z <= 3 - j
+
+    def block_at(mat, sign, j):
+        return weights.at[mat, block_rows((z - sign * j) * 2 + x)]
+
+    def weights_on(mat, j):
+        for sign in (1, -1):
+            here = arrives(sign, j)
+            rows = block_at(mat, sign, j)
+            onward = describe(z_index[mat, sign, j, "x"], rows, rows, x_peer)
+
+            @pl.when(here)
+            def _():
+                describe(z_index[mat, sign, j], rows, rows, x_peer).wait_recv()
+
+            if j < 3:
+                z_send_block(mat, sign, j + 1)
+
+            @pl.when(here)
+            def _():
+                onward.start()
+
+            later.append((here, onward))
 
     def weights_in(mat):
-        for k in (0, 1, 3, 2):
-            x_copies[mat, k].wait_recv()
+        own_x[mat].wait_recv()
+        for j in (1, 2, 3):
+            for sign in (1, -1):
+                rows = block_at(mat, sign, j)
+
+                @pl.when(arrives(sign, j))
+                def _():
+                    describe(z_index[mat, sign, j, "x"], rows, rows, x_peer).wait_recv()
 
     def norm_stats(rows):
         centre = rows - jnp.mean(rows, axis=-1, keepdims=True)
@@ -562,8 +603,8 @@
             - normal * jnp.mean(scaled * normal, axis=-1, keepdims=True)
         )
 
-    def first_norm(item):
-        @pl.loop(0, ROWS // 112)
+    def first_norm(item, low, high):
+        @pl.loop(low, high)
         def _(index):
             rows = pl.ds(pl.multiple_of(index * 112, 16), 112)
             normal, _ = norm_stats(tokens[item, rows, :].astype(F32))
@@ -571,11 +612,14 @@
 
     weights_out(0)
     loads[3].wait()
-    first_norm(far)
-    weights_on(0)
+    first_norm(0, 0, 4)
+    weights_on(0, 1)
+    first_norm(0, 4, 6)
+    first_norm(1, 0, 2)
+    weights_on(0, 2)
+    first_norm(1, 2, 6)
+    weights_on(0, 3)
     weights_out(1)
-    weights_out(2)
-    first_norm(y)
     loads[4].wait()
     zero_rows = jnp.zeros((KEYS - ROWS, HEAD_DIM), BF16)
     for i in range(6):
@@ -615,59 +659,59 @@
                 probs[at, first : first + HALF, 0:extent] = low
                 heads[at, first : first + HALF, :] = dot(low, values[at, 0:extent, :]).astype(BF16)
 
-    def join_heads(source, item, half):
-        rows = half_rows(half)
-        return jnp.concatenate([source[item * 3 + head, rows, :] for head in range(3)], axis=1)
-
-    def attention_out(item, slot):
+    def to_core(kind, item, source):
+        return send(source.at[item], kind.at[item], core_peer)
+
+    def to_swap(copy, kept, received, staged, swapped, item):
+        done_sending(copy)
+        copy.wait_recv()
+        staged[item] = (kept[item] + received[item].astype(F32)).astype(BF16)
+        return send(staged.at[item], swapped.at[item], y_peer)
+
+    def both(copy, staged, swapped, item):
+        copy.wait_recv()
+        return staged[item].astype(F32) + swapped[item].astype(F32)
+
+    def attention_out(item):
         for half in (0, 1):
-            context[item, half * HALF : (half + 1) * HALF, :] = join_heads(heads, item, half)
+            rows = slice(half * HALF, (half + 1) * HALF)
+            context[item, rows, :] = jnp.concatenate(
+                [heads[item * 3 + head, rows, :] for head in range(3)], axis=1
+            )
         outward = weights[0, :, 576:768]
-        send_a[slot] = dot(context[item, half_rows(1 - c), :], outward, NT).astype(BF16)
-        copy = send(send_a.at[slot], recv_attn.at[slot], core_peer)
-        keep[slot] = dot(context[item, half_rows(c), :], outward, NT)
+        send_a[item] = dot(context[item, half_rows(1 - c), :], outward, NT).astype(BF16)
+        copy = to_core(recv_one, item, send_a)
+        keep[item] = dot(context[item, mine, :], outward, NT)
         return copy
 
-    project(far)
-    attend(far)
-    attn_far = attention_out(far, 0)
-    project(y)
-    attn_far.wait_recv()
-    ysend_a[...] = (keep[0] + recv_attn[0].astype(F32)).astype(BF16)
-    attn_y = send(ysend_a, yrecv_attn, y_peer)
-    weights_on(1)
-    attend(y)
-    weights_on(2)
-    attn_near = attention_out(y, 1)
-    attn_near.wait_recv()
-    attn_y.wait_recv()
-    mine = half_rows(c)
-    middle[...] = (
-        tokens[y, mine, :].astype(F32)
-        + keep[1]
-        + recv_attn[1].astype(F32)
-        + yrecv_attn[...].astype(F32)
-    )
-    normal_two, _ = norm_stats(middle[...])
-    normed_two[y, mine, :] = (normal_two * norms[2:3, :] + norms[3:4, :]).astype(BF16)
-
-    def share_rows(buffer):
-        rows = buffer.at[y, mine]
-        return send(rows, rows, core_peer), send(rows, rows, y_peer)
-
-    def pass_on(buffer, copy):
-        copy.wait_recv()
-        rows = buffer.at[far, mine]
+    project(0)
+    weights_on(1, 1)
+    attend(0)
+    weights_on(1, 2)
+    attn_0 = attention_out(0)
+    weights_on(1, 3)
+    weights_out(2)
+    project(1)
+    swap_0 = to_swap(attn_0, keep, recv_one, send_a, swapped_one, 0)
+    weights_on(2, 1)
+    attend(1)
+    weights_on(2, 2)
+    attn_1 = attention_out(1)
+    weights_on(2, 3)
+    swap_1 = to_swap(attn_1, keep, recv_one, send_a, swapped_one, 1)
+
+    def share_rows(buffer, item):
+        rows = buffer.at[item, mine]
         return send(rows, rows, core_peer)
 
-    two_core, two_y = share_rows(normed_two)
-    weights_in(1)
-    weights_in(2)
-    done_sending(attn_far)
-    done_sending(attn_near)
-    done_sending(attn_y)
-
-    def feed_forward(item, half, keep_slot, send_slot):
+    def second_norm(copy, item):
+        rows = tokens[item, mine, :].astype(F32) + both(copy, send_a, swapped_one, item)
+        middle[item] = rows
+        normal, _ = norm_stats(rows)
+        normed_two[item, mine, :] = (normal * norms[2:3, :] + norms[3:4, :]).astype(BF16)
+        return share_rows(normed_two, item)
+
+    def feed_forward(item, half, keeps):
         rows = half_rows(half)
         upper = dot(normed_two[item, rows, :], weights[1])
         grown, slope = gelu_both(upper)
@@ -677,57 +721,57 @@
         grad_upper[item, rows, :] = pull
         terms = dot(pull, weights[1], NT)
         lowered = dot(grown, weights[2], NT)
-        if keep_slot is not None:
-            keep[keep_slot] = terms
-            keep_low[keep_slot] = lowered
+        if keeps:
+            keep[item] = terms
+            keep_low[item] = lowered
             return None
-        send_a[send_slot] = terms.astype(BF16)
-        first = send(send_a.at[send_slot], recv_mid.at[send_slot], core_peer)
-        send_b[send_slot] = lowered.astype(BF16)
-        return first, send(send_b.at[send_slot], recv_low.at[send_slot], core_peer)
-
-    feed_forward(y, c, 1, None)
-    two_core.wait_recv()
-    mid_near, low_near = feed_forward(y, 1 - c, None, 1)
-    two_on = pass_on(normed_two, two_y)
-    feed_forward(far, c, 0, None)
-    two_on.wait_recv()
-    mid_far, low_far = feed_forward(far, 1 - c, None, 0)
-    mid_far.wait_recv()
-    ysend_a[...] = (keep[0] + recv_mid[0].astype(F32)).astype(BF16)
-    mid_y = send(ysend_a, yrecv_mid, y_peer)
-    low_far.wait_recv()
-    ysend_b[...] = (keep_low[0] + recv_low[0].astype(F32)).astype(BF16)
-    low_y = send(ysend_b, yrecv_low, y_peer)
+        send_a[item] = terms.astype(BF16)
+        first = to_core(recv_mid, item, send_a)
+        send_b[item] = lowered.astype(BF16)
+        return first, to_core(recv_low, item, send_b)
+
+    two_0 = second_norm(swap_0, 0)
+    done_sending(swap_0)
+    weights_in(1)
+    weights_in(2)
+    feed_forward(0, c, True)
+    two_0.wait_recv()
+    mid_0, low_0 = feed_forward(0, 1 - c, False)
+    two_1 = second_norm(swap_1, 1)
+    done_sending(swap_1)
+    swap_mid_0 = to_swap(mid_0, keep, recv_mid, send_a, swapped_mid, 0)
+    feed_forward(1, c, True)
+    two_1.wait_recv()
+    mid_1, low_1 = feed_forward(1, 1 - c, False)
 
     def band_grad(slot, first, width, left_of, right_of):
         total[slot, :, first : first + width] = dot(left_of(0), right_of(0), TN) + dot(
             left_of(1), right_of(1), TN
         )
 
+    x_copies = {}
+    z_copies = {}
+
     def grads_out(mat, slot):
-        for k in range(4):
-            x_send[mat, k] = total[slot, block_rows(2 * k + 1 - x), :].astype(BF16)
-        return send(x_send.at[mat], x_recv.at[mat], x_peer)
-
-    def grads_on(mat, slot, copy):
-        copy.wait_recv()
-        sent = []
+        for k in (2, 1, 3, 0):
+            x_send[mat, k] = total[slot, block_rows(2 * ((z + k) % 4) + 1 - x), :].astype(BF16)
+            x_copies[mat, k] = send(x_send.at[mat, k], x_recv.at[mat, k], x_peer)
+
+    def grads_on(mat, slot):
         for k in (2, 1, 3):
-            other = (z + k) % 4
+            x_copies[mat, k].wait_recv()
             z_send[mat, k - 1] = (
-                total[slot, block_rows(2 * other + x), :] + x_recv[mat, other].astype(F32)
+                total[slot, block_rows(2 * ((z + k) % 4) + x), :] + x_recv[mat, k].astype(F32)
             ).astype(BF16)
-            sent.append(send(z_send.at[mat, k - 1], z_recv.at[mat, k - 1], z_peers[k - 1]))
-        shards_out[mat] = total[slot, own_block, :] + x_recv[mat, z].astype(F32)
-        return sent
-
-    def grads_in(mat, sent):
-        for copy in sent:
-            copy.wait_recv()
+            z_copies[mat, k] = send(z_send.at[mat, k - 1], z_recv.at[mat, k - 1], z_peers[k - 1])
+        x_copies[mat, 0].wait_recv()
+        shards_out[mat] = total[slot, own_block, :] + x_recv[mat, 0].astype(F32)
+
+    def grads_in(mat):
         summed = shards_out[mat]
-        for k in range(3):
-            summed += z_recv[mat, k].astype(F32)
+        for k in (1, 3, 2):
+            z_copies[mat, k].wait_recv()
+            summed += z_recv[mat, k - 1].astype(F32)
         shards_out[mat] = summed
         return jnp.sum(summed * summed)
 
@@ -736,36 +780,31 @@
             0, first, 256,
             lambda i: back[i], lambda i, f=first: hidden[i, :, f : f + 256],
         )
-    down_x = grads_out(2, 0)
+        if first == 0:
+            swap_mid_1 = to_swap(mid_1, keep, recv_mid, send_a, swapped_mid, 1)
+    grads_out(2, 0)
     for first in (0, 256, 512):
         band_grad(
             1, first, 256,
             lambda i: normed_two[i], lambda i, f=first: grad_upper[i, :, f : f + 256],
         )
-    up_x = grads_out(1, 1)
-
-    mid_near.wait_recv()
-    mid_y.wait_recv()
-    grad_two = keep[1] + recv_mid[1].astype(F32) + yrecv_mid[...].astype(F32)
-    normal_two, inverse_two = norm_stats(middle[...])
-    table_mine[2:3, :] = jnp.sum(grad_two * normal_two, axis=0, keepdims=True)
-    table_mine[3:4, :] = jnp.sum(grad_two, axis=0, keepdims=True)
-    grad_mid[...] = back[y, mine, :].astype(F32) + norm_back(
-        grad_two, normal_two, inverse_two, norms[2:3, :]
-    )
-    middle_low[y, mine, :] = grad_mid[...].astype(BF16)
-    ml_core, ml_y = share_rows(middle_low)
-
-    low_near.wait_recv()
-    low_y.wait_recv()
-    out_rows[y, mine, :] = (
-        middle[...] + keep_low[1] + recv_low[1].astype(F32) + yrecv_low[...].astype(F32)
-    ).astype(BF16)
-    out_core, out_y = share_rows(out_rows)
-    done_sending(mid_near)
-    done_sending(mid_far)
-    done_sending(mid_y)
-    down_z = grads_on(2, 0, down_x)
+    grads_out(1, 1)
+
+    def middle_back(copy, item):
+        grad_two = both(copy, send_a, swapped_mid, item)
+        normal, inverse = norm_stats(middle[item])
+        sums = (
+            jnp.sum(grad_two * normal, axis=0, keepdims=True),
+            jnp.sum(grad_two, axis=0, keepdims=True),
+        )
+        for row, part in zip((2, 3), sums):
+            table_mine[row : row + 1, :] = part if item == 0 else table_mine[row : row + 1, :] + part
+        pulled = back[item, mine, :].astype(F32) + norm_back(
+            grad_two, normal, inverse, norms[2:3, :]
+        )
+        grad_mid[item] = pulled
+        middle_low[item, mine, :] = pulled.astype(BF16)
+        return share_rows(middle_low, item)
 
     def attend_back(item):
         for half in (0, 1):
@@ -815,69 +854,80 @@
                 axis=1,
             )
 
-    def first_terms(item, slot):
+    def first_terms(item):
         inward = weights[0, :, 0:576]
-        send_a[slot] = dot(grad_triple[item, half_rows(1 - c), :], inward, NT).astype(BF16)
-        copy = send(send_a.at[slot], recv_first.at[slot], core_peer)
-        keep[slot] = dot(grad_triple[item, half_rows(c), :], inward, NT)
+        send_a[item] = dot(grad_triple[item, half_rows(1 - c), :], inward, NT).astype(BF16)
+        copy = to_core(recv_one, item, send_a)
+        keep[item] = dot(grad_triple[item, mine, :], inward, NT)
         return copy
 
-    ml_on = pass_on(middle_low, ml_y)
-    ml_on.wait_recv()
-    attend_back(far)
-    first_far = first_terms(far, 0)
-    up_z = grads_on(1, 1, up_x)
-    out_on = pass_on(out_rows, out_y)
-    first_far.wait_recv()
-    ysend_a[...] = (keep[0] + recv_first[0].astype(F32)).astype(BF16)
-    first_y = send(ysend_a, yrecv_first, y_peer)
-    ml_core.wait_recv()
-    attend_back(y)
-    first_near = first_terms(y, 1)
+    low_swap_0 = low_swap_1 = None
+    ml_0 = middle_back(swap_mid_0, 0)
+    done_sending(swap_mid_0)
+    ml_0.wait_recv()
+    attend_back(0)
+    first_0 = first_terms(0)
+    ml_1 = middle_back(swap_mid_1, 1)
+    done_sending(swap_mid_1)
+    first_swap_0 = to_swap(first_0, keep, recv_one, send_a, swapped_one, 0)
+    grads_on(2, 0)
+    ml_1.wait_recv()
+    attend_back(1)
+    first_1 = first_terms(1)
     for first, width in ((0, 256), (256, 256), (512, 64)):
         band_grad(
             0, first, width,
             lambda i: normed_one[i], lambda i, f=first, w=width: grad_triple[i, :, f : f + w],
         )
+        if first == 0:
+            first_swap_1 = to_swap(first_1, keep, recv_one, send_a, swapped_one, 1)
+            low_swap_0 = to_swap(low_0, keep_low, recv_low, send_b, swapped_low, 0)
+            low_swap_1 = to_swap(low_1, keep_low, recv_low, send_b, swapped_low, 1)
     band_grad(0, 576, 192, lambda i: middle_low[i], lambda i: context[i])
-    in_x = grads_out(0, 0)
-
-    first_near.wait_recv()
-    first_y.wait_recv()
-    grad_one = keep[1] + recv_first[1].astype(F32) + yrecv_first[...].astype(F32)
-    normal_one, inverse_one = norm_stats(tokens[y, mine, :].astype(F32))
-    table_mine[0:1, :] = jnp.sum(grad_one * normal_one, axis=0, keepdims=True)
-    table_mine[1:2, :] = jnp.sum(grad_one, axis=0, keepdims=True)
-    grad_rows[y, mine, :] = (
-        grad_mid[...] + norm_back(grad_one, normal_one, inverse_one, norms[0:1, :])
-    ).astype(BF16)
-    rows_core, rows_y = share_rows(grad_rows)
-
-    out_core.wait_recv()
-    out_on.wait_recv()
-    store_out = pltpu.make_async_copy(out_rows, output_h, local_sems.at[5])
-    store_out.start()
-    in_z = grads_on(0, 0, in_x)
-    squares = grads_in(2, down_z) + grads_in(1, up_z)
-    rows_on = pass_on(grad_rows, rows_y)
-    squares += grads_in(0, in_z)
+    grads_out(0, 0)
+    grads_on(1, 1)
+
+    stores = []
+
+    def give(half_buffer, result, item):
+        here = result.at[item, mine]
+        store = pltpu.make_async_copy(half_buffer.at[item], here, local_sems.at[5 + len(stores)])
+        store.start()
+        stores.append(store)
+        return send(half_buffer.at[item], here, core_peer)
+
+    def first_back(copy, item):
+        grad_one = both(copy, send_a, swapped_one, item)
+        normal, inverse = norm_stats(tokens[item, mine, :].astype(F32))
+        sums = (
+            jnp.sum(grad_one * normal, axis=0, keepdims=True),
+            jnp.sum(grad_one, axis=0, keepdims=True),
+        )
+        for row, part in zip((0, 1), sums):
+            table_mine[row : row + 1, :] = part if item == 0 else table_mine[row : row + 1, :] + part
+        grad_half[item] = (
+            grad_mid[item] + norm_back(grad_one, normal, inverse, norms[0:1, :])
+        ).astype(BF16)
+        return give(grad_half, grad_h, item)
+
+    rows_0 = first_back(first_swap_0, 0)
+    squares = grads_in(2)
+    grads_on(0, 0)
+    rows_1 = first_back(first_swap_1, 1)
+    squares += grads_in(1)
+    squares += grads_in(0)
     table_mine[4:8, :] = jnp.broadcast_to(squares, (4, table_mine.shape[1]))
 
-    rows_core.wait_recv()
-    rows_on.wait_recv()
-    store_rows = pltpu.make_async_copy(grad_rows, grad_h, local_sems.at[6])
-    store_rows.start()
-
-    at_hop = 0
-    for peer in (core_peer, y_peer, x_peer):
-        hop = send(table_mine, table_recv.at[at_hop], peer)
+    for hop_number, peer in enumerate((core_peer, y_peer, x_peer)):
+        hop = send(table_mine, table_recv.at[hop_number], peer)
         hop.wait_recv()
         done_sending(hop)
-        table_mine[...] = table_mine[...] + table_recv[at_hop]
-        at_hop += 1
-    hops = []
-    for k in (1, 2, 3):
-        hops.append(send(table_mine, table_recv.at[2 + k], z_peers[k - 1]))
+        received = table_recv[hop_number]
+        if hop_number == 1:
+            table_mine[4:8, :] = table_mine[4:8, :] + received[4:8]
+        else:
+            table_mine[...] = table_mine[...] + received
+    hops = [send(table_mine, table_recv.at[2 + k], z_peers[k - 1]) for k in (1, 2, 3)]
     for hop in hops:
         hop.wait_recv()
     parts = [table_mine[...], table_recv[3], table_recv[4], table_recv[5]]
@@ -889,10 +939,21 @@
         ordered = piece if ordered is None else ordered + piece
     table_out[...] = ordered
 
-    store_out.wait()
-    store_rows.wait()
+    given = [rows_0, rows_1]
+    for item, copy in ((0, low_swap_0), (1, low_swap_1)):
+        out_half[item] = (middle[item] + both(copy, send_b, swapped_low, item)).astype(BF16)
+        given.append(give(out_half, output_h, item))
+    for copy in given:
+        copy.wait_recv()
+    for store in stores:
+        store.wait()
     for copy in list(pending):
         copy.wait_send()
+    for wanted, copy in later:
+
+        @pl.when(wanted)
+        def _():
+            copy.wait_send()
 
 
 def fused_body(
@@ -918,7 +979,6 @@
     smem = pl.BlockSpec(memory_space=pltpu.SMEM)
     rows = pltpu.VMEM((2, ROWS, width), BF16)
     halves = pltpu.VMEM((2, HALF, width), BF16)
-    half = pltpu.VMEM((HALF, width), BF16)
     keep = pltpu.VMEM((2, HALF, width), F32)
     output, grads, shards, table = pl.pallas_call(
         fused_kernel,
@@ -941,28 +1001,24 @@
             pltpu.VMEM((6, ROWS, KEYS), BF16),
             pltpu.VMEM((6, ROWS, HEAD_DIM), BF16),
             pltpu.VMEM((2, ROWS, 192), BF16),
-            pltpu.VMEM((HALF, width), F32),
+            keep,
             rows,
             rows,
             rows,
             rows,
-            rows,
-            rows,
+            halves,
+            halves,
             keep,
             keep,
             halves,
             halves,
-            half,
-            half,
             halves,
             halves,
             halves,
             halves,
-            half,
-            half,
-            half,
-            half,
-            pltpu.VMEM((HALF, width), F32),
+            halves,
+            halves,
+            keep,
             pltpu.VMEM((2, ROWS, 576), BF16),
             pltpu.VMEM((2, width, width), F32),
             pltpu.VMEM((3, 4, block, width), BF16),
@@ -973,7 +1029,7 @@
             pltpu.VMEM((6, 8, width), F32),
             pltpu.SemaphoreType.DMA((N_REMOTE,)),
             pltpu.SemaphoreType.DMA((N_REMOTE,)),
-            pltpu.SemaphoreType.DMA((7,)),
+            pltpu.SemaphoreType.DMA((9,)),
         ],
         compiler_params=pltpu.CompilerParams(
             collective_id=0, has_side_effects=True, vmem_limit_bytes=VMEM_BYTES

time: 191 us -> 168 us (0.88)
  Pallas kernels: 164 us -> 141 us
    pallas_call x1, Pallas kernels: 164 us -> 141 us  [fused_body(): pl.pallas_call(fused_kernel, out_shape=(jax.ShapeDtypeStruct((2, ROWS, wi...]
where the time goes in v2:
time: 168 us; the launch traced here: 167 us
  Pallas kernels  141 us (84%)
  other arithmetic  11.6 us (7%)
  local copies, waits for them, and re-layouts  11 us (7%)
  between operations  3.39 us (2%)
    pallas_call x1, Pallas kernels, fused_body(): pl.pallas_call(fused_kernel, out_shape=(jax.ShapeDtypeStruct((2, ROWS, wi...  141 us
    sub x5, other arithmetic, adam_update(): master - step_rate * (first_hat / (jnp.sqrt(second_hat) + ADAM_EPSILON) +...  4.68 us
    unnamed x46, local copies, waits for them, and re-layouts  4.34 us

profile of v2, /device:TPU:0, one launch (start us, length us, event | category | flops | bytes accessed | tf_op | source)
XLA Modules:
  0.0 167.2 jit_solution(10227684083239816650)
XLA Ops:
  0.7 1.1 convert_bitcast_fusion
  1.8 1.0 convert_bitcast_fusion.1
  2.8 1.0 copy.37
  3.8 0.0 copy-start.7
  3.8 1.0 convert.26
  4.8 0.1 maximum_bitcast_fusion
  4.9 0.8 pad_maximum_fusion.shard_h
  5.8 1.4 pad.7.tokens_h
  7.2 0.9 copy-done.1
  8.1 1.5 pad.8.back_h
  9.5 141.2 %block_step.1 = (bf16[2,672,768]{2,1,0:T(8,128)(2,1)}, bf16[2,672,768]{2,1,0:T(8,128)(2,1)}, f32[3,96,768]{2,1,0:T(8,128)}, f32[8,768]{1,0:T(8,128)}) custom-call(s32[2]{0:T(128)} %steps.1, s32[2]{0:T(128)} %flags.1, bf16[3,96,768]{2,1,0:T(8,128)(2,1)} %pad_maximum_fusion.shard_h, bf16[2,672,768]{2,1,0:T(8,128)(2,1)} %pad.7.tokens_h, ...), custom_call_target="tpu_custom_call" | custom-call | tf_op jit(solution)/shard_map/block_step/pallas_call | solution.py:983
  150.8 3.1 %slice.45 = bf16[2,664,768]{2,1,0:T(8,128)(2,1)} slice(bf16[2,672,768]{2,1,0:T(8,128)(2,1)} %get-tuple-element.22), slice={[0:2], [0:664], [0:768]} | slice | bytes 4079616 | tf_op jit(solution)/shard_map/slice | solution.py:1066
  153.9 0.0 copy-start.9
  154.0 0.0 copy-start.10
  154.0 2.3 %slice_convert_fusion = f32[2,664,768]{2,1,0:T(8,128)} fusion(bf16[2,672,768]{2,1,0:T(8,128)(2,1)S(1)} %copy-done.2), kind=kLoop, calls=%fused_computation | loop fusion | flops 1019904 | bytes 6119424 | tf_op jit(solution)/shard_map/convert_element_type | solution.py:1067
  156.2 0.5 slice.47
  156.8 0.6 fusion.17
  158.8 0.0 copy-start.4
  158.8 0.0 copy-start.11
  158.8 0.0 copy-start.12
  158.8 0.1 fusion.16
  158.9 1.1 multiply_subtract_fusion.2
  160.0 0.1 copy.39
  160.1 0.1 copy.38
  160.2 0.2 multiply_subtract_fusion.3
  160.3 0.7 copy.42
  161.1 0.7 copy.43
  161.8 0.7 copy.44
  162.6 0.0 copy-start.19
  162.6 1.1 multiply_subtract_fusion.1
  163.7 1.1 multiply_subtract_fusion
  164.7 1.4 multiply_subtract_fusion.4
  (34 shorter events, 0.1 us)
Async XLA Ops:
  0.7 5.1 %copy-start = (bf16[2,664,768]{2,1,0:T(8,128)(2,1)S(1)}, bf16[2,664,768]{2,1,0:T(8,128)(2,1)}, u32[]{:S(2)}) copy-start(bf16[2,664,768]{2,1,0:T(8,128)(2,1)} %param.19) | copy-start | bytes 6119428
  3.8 3.4 %copy-start.7 = (f32[192,96]{0,1:T(8,128)}, f32[192,96]{0,1:T(8,128)S(1)}, u32[]{:S(2)}) copy-start(f32[192,96]{0,1:T(8,128)S(1)} %copy.37) | copy-start | bytes 221188
  5.8 2.3 %copy-start.1 = (bf16[2,664,768]{2,1,0:T(8,128)(2,1)S(1)}, bf16[2,664,768]{2,1,0:T(8,128)(2,1)}, u32[]{:S(2)}) copy-start(bf16[2,664,768]{2,1,0:T(8,128)(2,1)} %param.20) | copy-start | bytes 6119428
  150.8 3.2 %copy-start.2 = (bf16[2,672,768]{2,1,0:T(8,128)(2,1)S(1)}, bf16[2,672,768]{2,1,0:T(8,128)(2,1)}, u32[]{:S(2)}) copy-start(bf16[2,672,768]{2,1,0:T(8,128)(2,1)} %get-tuple-element.23) | copy-start | bytes 6193156
  153.9 2.3 %copy-start.17 = (f32[8,768]{1,0:T(8,128)S(1)}, f32[8,768]{1,0:T(8,128)}, u32[]{:S(2)}) copy-start(f32[8,768]{1,0:T(8,128)} %get-tuple-element.24) | copy-start | bytes 73732
  153.9 4.8 %copy-start.6 = (f32[3,96,768]{2,1,0:T(8,128)S(1)}, f32[3,96,768]{2,1,0:T(8,128)}, u32[]{:S(2)}) copy-start(f32[3,96,768]{2,1,0:T(8,128)} %get-tuple-element.25) | copy-start | bytes 2654212
  153.9 4.9 %copy-start.3 = (f32[3,96,192]{2,1,0:T(8,128)S(1)}, f32[3,96,192]{2,1,0:T(8,128)}, u32[]{:S(2)}) copy-start(f32[3,96,192]{2,1,0:T(8,128)} %param.23) | copy-start | bytes 663556
  153.9 4.9 %copy-start.9 = (f32[3,96,192]{2,1,0:T(8,128)S(1)}, f32[3,96,192]{2,1,0:T(8,128)}, u32[]{:S(2)}) copy-start(f32[3,96,192]{2,1,0:T(8,128)} %param.33) | copy-start | bytes 663556
  154.0 4.9 %copy-start.10 = (f32[3,96,192]{2,1,0:T(8,128)S(1)}, f32[3,96,192]{2,1,0:T(8,128)}, u32[]{:S(2)}) copy-start(f32[3,96,192]{2,1,0:T(8,128)} %param.28) | copy-start | bytes 663556
  156.2 3.7 %copy-start.15 = (f32[192,96]{1,0:T(8,128)S(1)}, f32[192,96]{1,0:T(8,128)}, u32[]{:S(2)}) copy-start(f32[192,96]{1,0:T(8,128)} %param.34) | copy-start | bytes 221188
  156.2 3.8 %copy-start.16 = (f32[192,96]{1,0:T(8,128)S(1)}, f32[192,96]{1,0:T(8,128)}, u32[]{:S(2)}) copy-start(f32[192,96]{1,0:T(8,128)} %param.29) | copy-start | bytes 221188
  156.2 3.9 %copy-start.8 = (f32[192,96]{0,1:T(8,128)S(1)}, f32[192,96]{0,1:T(8,128)}, u32[]{:S(2)}) copy-start(f32[192,96]{0,1:T(8,128)} %copy-done.7) | copy-start | bytes 221188
  158.8 3.8 %copy-start.4 = (f32[96,768]{1,0:T(8,128)S(1)}, f32[96,768]{1,0:T(8,128)}, u32[]{:S(2)}) copy-start(f32[96,768]{1,0:T(8,128)} %param.25) | copy-start | bytes 884740
  158.8 3.8 %copy-start.11 = (f32[96,768]{1,0:T(8,128)S(1)}, f32[96,768]{1,0:T(8,128)}, u32[]{:S(2)}) copy-start(f32[96,768]{1,0:T(8,128)} %param.35) | copy-start | bytes 884740
  158.8 3.8 %copy-start.12 = (f32[96,768]{1,0:T(8,128)S(1)}, f32[96,768]{1,0:T(8,128)}, u32[]{:S(2)}) copy-start(f32[96,768]{1,0:T(8,128)} %param.30) | copy-start | bytes 884740
  160.0 3.7 %copy-start.5 = (f32[768,96]{0,1:T(8,128)S(1)}, f32[768,96]{0,1:T(8,128)}, u32[]{:S(2)}) copy-start(f32[768,96]{0,1:T(8,128)} %param.26) | copy-start | bytes 884740
  160.0 3.7 %copy-start.13 = (f32[768,96]{0,1:T(8,128)S(1)}, f32[768,96]{0,1:T(8,128)}, u32[]{:S(2)}) copy-start(f32[768,96]{0,1:T(8,128)} %param.36) | copy-start | bytes 884740
  160.0 3.7 %copy-start.14 = (f32[768,96]{0,1:T(8,128)S(1)}, f32[768,96]{0,1:T(8,128)}, u32[]{:S(2)}) copy-start(f32[768,96]{0,1:T(8,128)} %param.31) | copy-start | bytes 884740
  162.6 2.1 %copy-start.18 = (f32[4,96]{1,0:T(4,128)S(1)}, f32[4,96]{1,0:T(4,128)}, u32[]{:S(2)}) copy-start(f32[4,96]{1,0:T(4,128)} %param.37) | copy-start | bytes 4612
  162.6 2.1 %copy-start.19 = (f32[4,96]{1,0:T(4,128)S(1)}, f32[4,96]{1,0:T(4,128)}, u32[]{:S(2)}) copy-start(f32[4,96]{1,0:T(4,128)} %param.32) | copy-start | bytes 4612

commit v3 on v2

--- a/solution.py
+++ b/solution.py
@@ -459,14 +459,14 @@
 
 
 def fused_kernel(
-    steps, flags, shard_h, tokens_h, back_h, norms,
+    steps, flags, inward_h, outward_h, upward_h, downward_h, tokens_h, back_h, norms,
     output_h, grad_h, shards_out, table_out,
     weights, tokens, back, normed_one, queries, keys, values, probs, heads, context,
     middle, normed_two, hidden, grad_upper, middle_low, out_half, grad_half,
     keep, keep_low, send_a, send_b,
     recv_one, recv_mid, recv_low, swapped_one, swapped_mid, swapped_low,
-    grad_mid, grad_triple, total, x_send, x_recv, z_send, z_recv,
-    table_mine, table_recv,
+    grad_mid, grad_triple, total, x_send, x_recv, z_recv,
+    table_mine, table_recv, inward_f, outward_f, upward_f, downward_f,
     send_sems, recv_sems, local_sems,
 ):
     dp = lax.axis_index("dp")
@@ -509,17 +509,29 @@
     mine = half_rows(c)
     own_block = block_rows(dp)
     loads = [
-        pltpu.make_async_copy(shard_h.at[i], weights.at[i, own_block], local_sems.at[i])
-        for i in range(3)
+        pltpu.make_async_copy(source, target, local_sems.at[4 + i])
+        for i, (source, target) in enumerate(
+            (
+                (inward_h, inward_f),
+                (outward_h, outward_f),
+                (upward_h, upward_f),
+                (downward_h, downward_f),
+                (tokens_h, tokens),
+                (back_h, back),
+            )
+        )
     ]
-    loads.append(pltpu.make_async_copy(tokens_h, tokens, local_sems.at[3]))
-    loads.append(pltpu.make_async_copy(back_h, back, local_sems.at[4]))
     for load in loads:
         load.start()
 
     barrier = pltpu.get_barrier_semaphore()
     for peer in all_peers:
         pl.semaphore_signal(barrier, inc=1, device_id=peer, device_id_type=MESH)
+    loads[0].wait()
+    loads[1].wait()
+    weights[0, own_block, :] = jnp.concatenate(
+        [inward_f[0], inward_f[1], inward_f[2], outward_f[...].T], axis=1
+    ).astype(BF16)
     pl.semaphore_wait(barrier, len(all_peers))
 
     later = []
@@ -549,7 +561,6 @@
         later.append((wanted, copy))
 
     def weights_out(mat):
-        loads[mat].wait()
         for sign in (1, -1):
             z_send_block(mat, sign, 1)
         rows = weights.at[mat, own_block]
@@ -603,15 +614,30 @@
             - normal * jnp.mean(scaled * normal, axis=-1, keepdims=True)
         )
 
+    def load_half(source, item, half):
+        body = source[item, pl.ds(pl.multiple_of(half * HALF, 16), SLOTS - HALF), :].astype(F32)
+        tail = source[item, SLOTS - HALF : HALF, :].astype(F32)
+        return jnp.concatenate([body, jnp.where(half == 0, tail, 0.0)], axis=0)
+
     def first_norm(item, low, high):
-        @pl.loop(low, high)
+        @pl.loop(low, min(high, 5))
         def _(index):
             rows = pl.ds(pl.multiple_of(index * 112, 16), 112)
             normal, _ = norm_stats(tokens[item, rows, :].astype(F32))
             normed_one[item, rows, :] = (normal * norms[0:1, :] + norms[1:2, :]).astype(BF16)
 
+        if high == 6:
+            normal, _ = norm_stats(tokens[item, 560:SLOTS, :].astype(F32))
+            normed = normal * norms[0:1, :] + norms[1:2, :]
+            none = jnp.zeros((ROWS - SLOTS, normed.shape[1]), F32)
+            normed_one[item, 560:ROWS, :] = jnp.concatenate([normed, none], axis=0).astype(BF16)
+
     weights_out(0)
+    loads[2].wait()
     loads[3].wait()
+    weights[1, own_block, :] = upward_f[...].astype(BF16)
+    weights[2, own_block, :] = downward_f[...].astype(BF16)
+    loads[4].wait()
     first_norm(0, 0, 4)
     weights_on(0, 1)
     first_norm(0, 4, 6)
@@ -620,7 +646,7 @@
     first_norm(1, 2, 6)
     weights_on(0, 3)
     weights_out(1)
-    loads[4].wait()
+    loads[5].wait()
     zero_rows = jnp.zeros((KEYS - ROWS, HEAD_DIM), BF16)
     for i in range(6):
         keys[i, ROWS:KEYS, :] = zero_rows
@@ -705,7 +731,7 @@
         return send(rows, rows, core_peer)
 
     def second_norm(copy, item):
-        rows = tokens[item, mine, :].astype(F32) + both(copy, send_a, swapped_one, item)
+        rows = load_half(tokens, item, c) + both(copy, send_a, swapped_one, item)
         middle[item] = rows
         normal, _ = norm_stats(rows)
         normed_two[item, mine, :] = (normal * norms[2:3, :] + norms[3:4, :]).astype(BF16)
@@ -717,7 +743,7 @@
         grown, slope = gelu_both(upper)
         grown = grown.astype(BF16)
         hidden[item, rows, :] = grown
-        pull = (dot(back[item, rows, :], weights[2]) * slope).astype(BF16)
+        pull = (dot(load_half(back, item, half).astype(BF16), weights[2]) * slope).astype(BF16)
         grad_upper[item, rows, :] = pull
         terms = dot(pull, weights[1], NT)
         lowered = dot(grown, weights[2], NT)
@@ -759,11 +785,12 @@
 
     def grads_on(mat, slot):
         for k in (2, 1, 3):
+            done_sending(x_copies[mat, k])
             x_copies[mat, k].wait_recv()
-            z_send[mat, k - 1] = (
+            x_send[mat, k] = (
                 total[slot, block_rows(2 * ((z + k) % 4) + x), :] + x_recv[mat, k].astype(F32)
             ).astype(BF16)
-            z_copies[mat, k] = send(z_send.at[mat, k - 1], z_recv.at[mat, k - 1], z_peers[k - 1])
+            z_copies[mat, k] = send(x_send.at[mat, k], z_recv.at[mat, k - 1], z_peers[k - 1])
         x_copies[mat, 0].wait_recv()
         shards_out[mat] = total[slot, own_block, :] + x_recv[mat, 0].astype(F32)
 
@@ -778,7 +805,7 @@
     for first in (0, 256, 512):
         band_grad(
             0, first, 256,
-            lambda i: back[i], lambda i, f=first: hidden[i, :, f : f + 256],
+            lambda i: back[i], lambda i, f=first: hidden[i, 0:SLOTS, f : f + 256],
         )
         if first == 0:
             swap_mid_1 = to_swap(mid_1, keep, recv_mid, send_a, swapped_mid, 1)
@@ -799,7 +826,7 @@
         )
         for row, part in zip((2, 3), sums):
             table_mine[row : row + 1, :] = part if item == 0 else table_mine[row : row + 1, :] + part
-        pulled = back[item, mine, :].astype(F32) + norm_back(
+        pulled = load_half(back, item, c) + norm_back(
             grad_two, normal, inverse, norms[2:3, :]
         )
         grad_mid[item] = pulled
@@ -891,14 +918,14 @@
 
     def give(half_buffer, result, item):
         here = result.at[item, mine]
-        store = pltpu.make_async_copy(half_buffer.at[item], here, local_sems.at[5 + len(stores)])
+        store = pltpu.make_async_copy(half_buffer.at[item], here, local_sems.at[len(stores)])
         store.start()
         stores.append(store)
         return send(half_buffer.at[item], here, core_peer)
 
     def first_back(copy, item):
         grad_one = both(copy, send_a, swapped_one, item)
-        normal, inverse = norm_stats(tokens[item, mine, :].astype(F32))
+        normal, inverse = norm_stats(load_half(tokens, item, c))
         sums = (
             jnp.sum(grad_one * normal, axis=0, keepdims=True),
             jnp.sum(grad_one, axis=0, keepdims=True),
@@ -956,6 +983,88 @@
             copy.wait_send()
 
 
+def update_kernel(
+    place, output_h, grad_h, shards_h, table_h, norms_h, *refs
+):
+    params_h, results, scratch = refs[:14], refs[14:32], refs[32:]
+    output_to, grad_to, norm_out = results[:3]
+    targets = results[3:]
+    output_in, grad_in, output_v, grad_v, shards, table, norms = scratch[:7]
+    params = scratch[7:21]
+    updated = scratch[21:36]
+    load_sems, store_sems = scratch[36:]
+    loads = [
+        pltpu.make_async_copy(source, target, load_sems.at[i])
+        for i, (source, target) in enumerate(
+            zip(
+                (table_h, grad_h, output_h, shards_h, norms_h) + params_h,
+                (table, grad_in, output_in, shards, norms) + params,
+            )
+        )
+    ]
+    for load in loads:
+        load.start()
+    stores = []
+
+    def store(source, target):
+        copy = pltpu.make_async_copy(source, target, store_sems.at[len(stores)])
+        copy.start()
+        stores.append(copy)
+
+    loads[0].wait()
+    sums = table[0:4, :]
+    total = table[4:5, 0:1] + jnp.sum(
+        jnp.sum(sums * sums, axis=1, keepdims=True), axis=0, keepdims=True
+    )
+    grad_norm = jnp.sqrt(total)
+    norm_out[...] = grad_norm
+    clip = jnp.minimum(1.0, CLIP_NORM / (grad_norm + 1e-06))
+
+    loads[1].wait()
+    for item in range(2):
+        grad_v[item] = grad_in[item, 0:SLOTS, :].astype(F32)
+        store(grad_v.at[item], grad_to.at[item])
+    loads[2].wait()
+    output_v[...] = output_in[:, 0:SLOTS, :]
+    store(output_v, output_to)
+    loads[3].wait()
+    loads[4].wait()
+
+    def update(index, gradients, rate, decay, master_at=None):
+        m_at, v_at = 4 + index, 9 + index
+        for at in (m_at, v_at) if index == 4 else (index, m_at, v_at):
+            loads[5 + at].wait()
+        for part, gradient in enumerate(gradients):
+            at = (lambda ref: ref.at[part]) if index == 0 else (lambda ref: ref)
+            master = master_at if index == 4 else at(params[index])[...]
+            values = adam_update(
+                master, at(params[m_at])[...], at(params[v_at])[...], gradient, clip, rate, decay
+            )
+            for which, value in enumerate(values):
+                at(updated[3 * index + which])[...] = value
+        for which in range(3):
+            store(updated[3 * index + which], targets[3 * index + which])
+
+    part = params[0].shape[2]
+    update(3, [shards[2]], RATE_DOWNWARD, WEIGHT_DECAY)
+    update(2, [shards[1]], RATE_UPWARD, WEIGHT_DECAY)
+    update(
+        0, [shards[0, :, i * part : (i + 1) * part] for i in range(3)], RATE_INWARD, WEIGHT_DECAY
+    )
+    update(1, [shards[0, :, 3 * part :].T], RATE_OUTWARD, WEIGHT_DECAY)
+    span = params[8].shape[1]
+    own_sums = sums[:, 0:span]
+    own_norms = norms[:, 0:span]
+    for index in range(1, 8):
+        here = place[0] == index
+        columns = slice(index * span, (index + 1) * span)
+        own_sums = jnp.where(here, sums[:, columns], own_sums)
+        own_norms = jnp.where(here, norms[:, columns], own_norms)
+    update(4, [own_sums], RATE_NORMS, 0.0, own_norms)
+    for copy in stores:
+        copy.wait()
+
+
 def fused_body(
     tokens, cotangent, step_counts, wrist_flags,
     inward_weight, outward_weight, upward_weight, downward_weight, norm_table,
@@ -964,16 +1073,6 @@
 ):
     width = norm_table.shape[1]
     block = upward_weight.shape[0]
-    shard = jnp.stack(
-        [
-            jnp.concatenate(
-                [inward_weight[0], inward_weight[1], inward_weight[2], outward_weight.T], axis=1
-            ),
-            upward_weight,
-            downward_weight.T,
-        ]
-    ).astype(BF16)
-    padding = ((0, 0), (0, ROWS - SLOTS), (0, 0))
     any_spec = pl.BlockSpec(memory_space=pl.ANY)
     vmem = pl.BlockSpec(memory_space=pltpu.VMEM)
     smem = pl.BlockSpec(memory_space=pltpu.SMEM)
@@ -988,12 +1087,12 @@
             jax.ShapeDtypeStruct((3, block, width), F32),
             jax.ShapeDtypeStruct((8, width), F32),
         ),
-        in_specs=[smem, smem, any_spec, any_spec, any_spec, vmem],
+        in_specs=[smem, smem, any_spec, any_spec, any_spec, any_spec, any_spec, any_spec, vmem],
         out_specs=(any_spec, any_spec, vmem, vmem),
         scratch_shapes=[
             pltpu.VMEM((3, width, width), BF16),
-            rows,
-            rows,
+            pltpu.VMEM((2, SLOTS, width), BF16),
+            pltpu.VMEM((2, SLOTS, width), BF16),
             rows,
             pltpu.VMEM((6, ROWS, HEAD_DIM), BF16),
             pltpu.VMEM((6, KEYS, HEAD_DIM), BF16),
@@ -1024,12 +1123,15 @@
             pltpu.VMEM((3, 4, block, width), BF16),
             pltpu.VMEM((3, 4, block, width), BF16),
             pltpu.VMEM((3, 3, block, width), BF16),
-            pltpu.VMEM((3, 3, block, width), BF16),
             pltpu.VMEM((8, width), F32),
             pltpu.VMEM((6, 8, width), F32),
+            pltpu.VMEM(inward_weight.shape, F32),
+            pltpu.VMEM(outward_weight.shape, F32),
+            pltpu.VMEM(upward_weight.shape, F32),
+            pltpu.VMEM(upward_weight.shape, F32),
             pltpu.SemaphoreType.DMA((N_REMOTE,)),
             pltpu.SemaphoreType.DMA((N_REMOTE,)),
-            pltpu.SemaphoreType.DMA((9,)),
+            pltpu.SemaphoreType.DMA((10,)),
         ],
         compiler_params=pltpu.CompilerParams(
             collective_id=0, has_side_effects=True, vmem_limit_bytes=VMEM_BYTES
@@ -1038,36 +1140,53 @@
     )(
         step_counts,
         wrist_flags,
-        shard,
-        jnp.pad(tokens, padding),
-        jnp.pad(cotangent, padding),
+        inward_weight,
+        outward_weight,
+        upward_weight,
+        downward_weight.T,
+        tokens,
+        cotangent,
         norm_table,
     )
-    part = inward_weight.shape[2]
-    grad_inward = jnp.stack([shards[0, :, i * part : (i + 1) * part] for i in range(3)])
-    grad_outward = shards[0, :, 3 * part :].T
-    table_sums = table[:4]
-    grad_norm = jnp.sqrt(table[4, 0] + jnp.sum(table_sums * table_sums))
-    clip_scale = jnp.minimum(1.0, CLIP_NORM / (grad_norm + 1e-06))
-    shard_width = momentum_norms.shape[1]
-    start = lax.axis_index("dp") * shard_width
-    own_table = lax.dynamic_slice_in_dim(norm_table, start, shard_width, 1)
-    own_sums = lax.dynamic_slice_in_dim(table_sums, start, shard_width, 1)
-    updated = []
-    for master, momentum, variance, gradient, rate, decay in (
-        (inward_weight, momentum_inward, variance_inward, grad_inward, RATE_INWARD, WEIGHT_DECAY),
-        (outward_weight, momentum_outward, variance_outward, grad_outward, RATE_OUTWARD, WEIGHT_DECAY),
-        (upward_weight, momentum_upward, variance_upward, shards[1], RATE_UPWARD, WEIGHT_DECAY),
-        (downward_weight, momentum_downward, variance_downward, shards[2].T, RATE_DOWNWARD, WEIGHT_DECAY),
-        (own_table, momentum_norms, variance_norms, own_sums, RATE_NORMS, 0.0),
-    ):
-        updated.extend(adam_update(master, momentum, variance, gradient, clip_scale, rate, decay))
-    return (
-        output[:, :SLOTS],
-        grads[:, :SLOTS].astype(F32),
-        grad_norm,
-        *updated,
-    )
+    place = jnp.reshape(lax.axis_index("dp"), (1,)).astype(jnp.int32)
+    params = (
+        inward_weight, outward_weight, upward_weight, downward_weight.T,
+        momentum_inward, momentum_outward, momentum_upward, momentum_downward.T, momentum_norms,
+        variance_inward, variance_outward, variance_upward, variance_downward.T, variance_norms,
+    )
+    shapes = [param.shape for param in params]
+    updates = [shape for shape in shapes[:4] + shapes[8:9] for _ in range(3)]
+    padded = pltpu.VMEM((2, ROWS, width), BF16)
+    results = pl.pallas_call(
+        update_kernel,
+        out_shape=(
+            jax.ShapeDtypeStruct((2, SLOTS, width), BF16),
+            jax.ShapeDtypeStruct((2, SLOTS, width), F32),
+            jax.ShapeDtypeStruct((1, 1), F32),
+            *[jax.ShapeDtypeStruct(shape, F32) for shape in updates],
+        ),
+        in_specs=[smem] + [any_spec] * 19,
+        out_specs=(any_spec, any_spec, vmem) + (any_spec,) * 15,
+        scratch_shapes=[
+            padded,
+            padded,
+            pltpu.VMEM((2, SLOTS, width), BF16),
+            pltpu.VMEM((2, SLOTS, width), F32),
+            pltpu.VMEM((3, block, width), F32),
+            pltpu.VMEM((8, width), F32),
+            pltpu.VMEM((4, width), F32),
+            *[pltpu.VMEM(shape, F32) for shape in shapes],
+            *[pltpu.VMEM(shape, F32) for shape in updates],
+            pltpu.SemaphoreType.DMA((19,)),
+            pltpu.SemaphoreType.DMA((18,)),
+        ],
+        compiler_params=pltpu.CompilerParams(vmem_limit_bytes=VMEM_BYTES),
+        name="update_step",
+    )(place, output, grads, shards, table, norm_table, *params)
+    updated = list(results[3:])
+    for index in (9, 10, 11):
+        updated[index] = updated[index].T
+    return (results[0], results[1], results[2][0, 0], *updated)
 
 
 def solution(mesh):

time: 168 us -> 151 us (0.90)
  other arithmetic: 11.6 us -> 0 us
  local copies, waits for them, and re-layouts: 11 us -> 0 us
  Pallas kernels: 141 us -> 150 us
  between operations: 3.39 us -> 0.87 us
    pallas_call x0 -> x1, Pallas kernels: none -> 8.28 us  [fused_body(): pl.pallas_call(update_kernel, out_shape=(jax.ShapeDtypeStruct((2, SLOTS,...]
    sub x5 -> x0, other arithmetic: 4.68 us -> none  [adam_update(): master - step_rate * (first_hat / (jnp.sqrt(second_hat) + ADAM_EPSILON) +...]
    unnamed x46 -> x0, local copies, waits for them, and re-layouts: 4.34 us -> none
    another operation x5 -> x0, other arithmetic: 4.03 us -> none  [the longest x4 3.03 us: fused_body(): jnp.stack([jnp.concatenate([inward_weight[0], inward_weight[1], inward_we...]
    slice x3 -> x0, local copies, waits for them, and re-layouts: 3.75 us -> none  [the longest x1 3.15 us: fused_body(): output[:, :SLOTS]]
    pad x2 -> x0, local copies, waits for them, and re-layouts: 2.9 us -> none  [the longest x1 1.46 us: fused_body(): jnp.pad(cotangent, padding)]
    convert_element_type x1 -> x0, other arithmetic: 2.26 us -> none  [fused_body(): grads[:, :SLOTS].astype(F32)]
where the time goes in v3:
time: 151 us; the launch traced here: 150 us
  Pallas kernels  150 us (99%)
    pallas_call x1, Pallas kernels, fused_body(): pl.pallas_call(fused_kernel, out_shape=(jax.ShapeDtypeStruct((2, ROWS, wi...  141 us
    pallas_call x1, Pallas kernels, fused_body(): pl.pallas_call(update_kernel, out_shape=(jax.ShapeDtypeStruct((2, SLOTS,...  8.28 us

profile of v3, /device:TPU:0, one launch (start us, length us, event | category | flops | bytes accessed | tf_op | source)
XLA Modules:
  0.0 150.4 jit_solution(17124171098264243550)
XLA Ops:
  0.7 141.3 %block_step.1 = (bf16[2,672,768]{2,1,0:T(8,128)(2,1)}, bf16[2,672,768]{2,1,0:T(8,128)(2,1)}, f32[3,96,768]{2,1,0:T(8,128)}, f32[8,768]{1,0:T(8,128)}) custom-call(s32[2]{0:T(128)} %steps.1, s32[2]{0:T(128)} %flags.1, f32[3,96,192]{2,1,0:T(8,128)} %refs_0_.1, f32[192,96]{1,0:T(8,128)} %refs_1_.1, f32[96,768]{1,0:T(8,128)} %refs_2_.1, f32[96,768]{1,0:T(8,128)} %bitcast.8, ...), custom_call_target="tpu_custom_call" | custom-call | tf_op jit(solution)/shard_map/block_step/pallas_call | solution.py:1082
  141.9 8.3 %update_step.1 = (bf16[2,664,768]{2,1,0:T(8,128)(2,1)}, f32[2,664,768]{2,1,0:T(8,128)}, f32[1,1]{1,0:T(1,128)}, f32[3,96,192]{2,1,0:T(8,128)}, f32[3,96,192]{2,1...) custom-call(s32[1]{0:T(128)} %bitcast.place, ...), custom_call_target="tpu_custom_call" | custom-call | tf_op jit(solution)/shard_map/update_step/pallas_call | solution.py:1160
